TPU v7x, 256 devices: a whole 4x4x8 slice. The times are simulated.
256 devices in a mesh: dp: 16 (over x, y), expert: 16 (over z, core).
Axes of the slice: x: 4, y: 4, z: 8, core: 2. Of those that a mesh axis runs over, the one named last changes fastest.
Arguments:
- out_grad: bfloat16 [32768, 2048], P(('dp', 'expert')), may hold values from -5 to 5
- saved_hidden: bfloat16 [32768, 8, 384], P(('dp', 'expert')), may hold values from -6 to 6
- gate_weight: bfloat16 [32768, 8], P(('dp', 'expert')), may hold values from 0.19921875 to 1
- expert_ids: int32 [32768, 8], P(('dp', 'expert')), may hold values from 0 to 63, all different within a row; in each aligned block of 128 rows (0 to 127, 128 to 255, ...) at most 24 rows name the same one
- down_weight: bfloat16 [2048, 64, 384], P('dp', 'expert'), may hold values from -0.3125 to 0.3125
Outputs:
- grad_hidden: bfloat16 [32768, 8, 384], P(('dp', 'expert'))
- grad_gate: bfloat16 [32768, 8], P(('dp', 'expert'))
- grad_down: float32 [2048, 64, 384], P('dp', 'expert')
Inputs may be any that keep to these rules, and one draw needn't show every extreme that they name: `expert_ids`: each token names 8 different experts. Among the tokens of one device no expert is named by more than 24 tokens, and in every draw some expert is named by exactly 24 tokens of some device.
All inputs are finite; a program needn't handle non-finite values.
Results may differ from a plain program's by a relative error of at most 0.014.
Values may be sent and summed in bfloat16 or wider, within the bound.
No kernel may reach another device: no remote copies, remote signals or barrier semaphores. Data moves between devices by JAX's collectives and lax.ppermute only.
A program may use at most 128 MiB of HBM per device.

v0:
```python
import functools

import jax
import jax.numpy as jnp
from jax import lax
from jax.experimental import pallas as pl
from jax.experimental.pallas import tpu as pltpu
from jax.sharding import PartitionSpec as P

CAP = 24
SIDE = 4
EXTRA = 8
BF16, F32, I32 = jnp.bfloat16, jnp.float32, jnp.int32


def iota(shape, dim):
    return lax.broadcasted_iota(I32, shape, dim)


def dot(a, b):
    return jnp.dot(a, b, preferred_element_type=F32)


def pack_kernel(owners, local, ids_ref, gate_ref, hidden_ref, wire_ref, pos_ref):
    top, tokens = ids_ref.shape
    routes, width = hidden_ref.shape
    experts = owners * local
    ids = ids_ref[...]
    expert_no = iota((experts, tokens), 0)
    named = [expert_no == ids[k : k + 1, :] for k in range(top)]
    member = sum(n.astype(F32) for n in named)
    earlier = (iota((tokens, tokens), 0) < iota((tokens, tokens), 1)).astype(F32).astype(BF16)
    before = dot(member.astype(BF16), earlier)
    pos = jnp.concatenate(
        [jnp.sum(jnp.where(n, before, 0.0), axis=0, keepdims=True) for n in named], axis=0
    )
    pos_ref[...] = pos
    spread = (iota((tokens, routes), 1) // top == iota((tokens, routes), 0)).astype(F32).astype(BF16)
    own = iota((top, routes), 1) % top == iota((top, routes), 0)

    def row(x):
        return jnp.sum(jnp.where(own, dot(x.astype(BF16), spread), 0.0), axis=0, keepdims=True)

    slot_row = row(ids.astype(F32)) * CAP + row(pos)
    gate_row = row(gate_ref[...].astype(F32))
    slots = jnp.where(member > 0.0, before, -1.0).astype(BF16)
    r, c = iota((owners * EXTRA, experts), 0), iota((owners * EXTRA, experts), 1)
    pick = ((r % EXTRA < local) & (c == r // EXTRA * local + r % EXTRA)).astype(F32).astype(BF16)
    slots = dot(pick, slots)
    slots = jnp.concatenate([slots, jnp.zeros((owners * EXTRA, width - tokens), F32)], axis=1)
    rows = local * CAP
    group = 4
    hidden = hidden_ref[...]
    for g in range(owners // group):
        row_no = (iota((group * rows, routes), 0) + g * group * rows).astype(F32)
        onehot = jnp.where(row_no == slot_row, gate_row, 0.0).astype(BF16)
        packed = dot(onehot, hidden)
        for i in range(group):
            o = g * group + i
            wire_ref[o] = jnp.concatenate(
                [packed[i * rows : (i + 1) * rows], slots[o * EXTRA : (o + 1) * EXTRA]], axis=0
            ).astype(BF16)


def expert_kernel(local, at_ref, wire_ref, grad_hbm, *refs):
    half = local // 2
    pieces, refs = refs[: 2 * SIDE], refs[2 * SIDE :]
    messages, u_hbm = refs[: 2 * SIDE], refs[2 * SIDE]
    gbuf, xbuf, abuf, wbuf, ubuf, obuf, gsem, wsem, msem, usem = refs[2 * SIDE + 1 :]
    owners, tokens, model = gbuf.shape
    width = wire_ref.shape[2]
    depth = model // (SIDE * SIDE)
    chips = owners // 2
    loads = [
        pltpu.make_async_copy(grad_hbm.at[pl.ds(2 * p, 2)], gbuf.at[pl.ds(2 * p, 2)], gsem.at[p])
        for p in range(chips)
    ]
    weights = [
        [pltpu.make_async_copy(pieces[h * SIDE + a], wbuf.at[h, a], wsem.at[h, a]) for a in range(SIDE)]
        for h in range(2)
    ]
    for c in loads + weights[0] + weights[1]:
        c.start()
    places = []
    for d in range(SIDE * SIDE):
        dx = (d // SIDE + SIDE - at_ref[0]) % SIDE
        dy = (d % SIDE + SIDE - at_ref[1]) % SIDE
        places.append(pl.multiple_of((dx * SIDE + dy) * depth, depth))
    block = 2 * CAP
    for p in range(chips):
        slot = [
            wire_ref[2 * p + i, local * CAP : local * CAP + EXTRA, :tokens].astype(F32)
            for i in range(2)
        ]
        slot[1] = jnp.where(slot[1] >= 0.0, slot[1] + CAP, -1.0)
        slot = jnp.concatenate(slot, axis=1)
        onehot = jnp.concatenate(
            [
                (slot[e : e + 1, :] == iota((block, 2 * tokens), 0).astype(F32)).astype(F32)
                for e in range(local)
            ],
            axis=0,
        ).astype(BF16)
        loads[p].wait()
        rows = dot(onehot, gbuf[2 * p : 2 * p + 2].reshape(2 * tokens, model)).astype(BF16)
        for e in range(local):
            for d in range(SIDE * SIDE):
                xbuf[e, p * block : (p + 1) * block, pl.ds(places[d], depth)] = rows[
                    e * block : (e + 1) * block, d * depth : (d + 1) * depth
                ]
    copies = []
    wire = wire_ref[:, : local * CAP, :].astype(F32)
    step = SIDE * depth
    for e in range(local):
        hidden = wire[:, e * CAP : (e + 1) * CAP, :].reshape(owners * CAP, width)
        hidden = hidden.T.astype(BF16)
        h = e // half
        for dx in range(SIDE):
            grad = dot(hidden, xbuf[e, :, dx * step : (dx + 1) * step]).astype(BF16)
            for dy in range(SIDE):
                a, b = (dx, dy) if h == 0 else (dy, dx)
                abuf[h, a, b, e % half] = grad[:, dy * depth : (dy + 1) * depth]
        if e % half == half - 1:
            for a in range(SIDE):
                copies.append(
                    pltpu.make_async_copy(abuf.at[h, a], messages[h * SIDE + a], msem.at[h, a])
                )
                copies[-1].start()
    for e in range(local):
        h = e // half
        if e % half == 0:
            for c in weights[h]:
                c.wait()
        u = jnp.zeros((owners * CAP, width), F32)
        for dx in range(SIDE):
            w = wbuf[0, :, dx, e % half] if h == 0 else wbuf[1, dx, :, e % half]
            u += dot(xbuf[e, :, dx * step : (dx + 1) * step], w.reshape(step, width))
        ubuf[:, e * CAP : (e + 1) * CAP, :] = u.reshape(owners, CAP, width)
    obuf[...] = ubuf[...].astype(BF16)
    copies.append(pltpu.make_async_copy(obuf, u_hbm, usem))
    copies[-1].start()
    for c in copies:
        c.wait()


def unpack_kernel(ids_ref, pos_ref, gate_ref, hidden_ref, back_ref, out_ref, gate_out_ref):
    top, tokens = ids_ref.shape
    routes, width = hidden_ref.shape
    slots = back_ref.shape[0]
    spread = (iota((routes, tokens), 0) // top == iota((routes, tokens), 1)).astype(F32).astype(BF16)
    own = iota((routes, top), 0) % top == iota((routes, top), 1)

    def column(x):
        y = lax.dot_general(spread, x.astype(BF16), (((1,), (1,)), ((), ())), preferred_element_type=F32)
        return jnp.sum(jnp.where(own, y, 0.0), axis=1, keepdims=True)

    slot = column(ids_ref[...].astype(F32)) * CAP + column(pos_ref[...])
    gate = column(gate_ref[...].astype(F32))
    back = back_ref[...]
    part = routes // 4
    grads = []
    for p in range(4):
        here = slice(p * part, (p + 1) * part)
        onehot = (iota((part, slots), 1).astype(F32) == slot[here]).astype(F32).astype(BF16)
        rows = dot(onehot, back)
        out_ref[here, :] = (rows * gate[here]).astype(BF16)
        grads.append(jnp.sum(rows * hidden_ref[here, :].astype(F32), axis=1, keepdims=True))
    grad = jnp.where(own, jnp.concatenate(grads, axis=0), 0.0).astype(BF16)
    gate_out_ref[...] = lax.dot_general(
        grad, spread, (((0,), (0,)), ((), ())), preferred_element_type=F32
    ).astype(BF16)


def finish_kernel(*refs):
    out_ref = refs[-1]
    half = out_ref.shape[1] // 2
    for h in range(2):
        parts = refs[h * SIDE : (h + 1) * SIDE]
        for e in range(half):
            total = sum(p[e].astype(F32) for p in parts)
            out_ref[:, h * half + e, :] = total.T


def shift(x, axis, step):
    pairs = []
    for i in range(SIDE):
        for j in range(SIDE):
            to = ((i + step) % SIDE, j) if axis == 0 else (i, (j + step) % SIDE)
            pairs.append((i * SIDE + j, to[0] * SIDE + to[1]))
    return lax.ppermute(x, "dp", pairs)


def gather_half(weights, first):
    blocks = jnp.stack([weights] + [shift(weights, first, -d) for d in range(1, SIDE)])
    return [blocks] + [shift(blocks, 1 - first, -d) for d in range(1, SIDE)]


def add(*parts):
    return sum(p.astype(F32) for p in parts)


def scatter_half(messages, first):
    got = [messages[0]] + [shift(messages[d], first, d) for d in range(1, SIDE)]
    sums = [add(*[g[d] for g in got]).astype(BF16) for d in range(SIDE)]
    return [sums[0]] + [shift(sums[d], 1 - first, d) for d in range(1, SIDE)]


VMEM = pl.BlockSpec(memory_space=pltpu.VMEM)
SMEM = pl.BlockSpec(memory_space=pltpu.SMEM)
ANY = pl.BlockSpec(memory_space=pl.ANY)
HBM = pl.BlockSpec(memory_space=pltpu.HBM)


def params(mib):
    return pltpu.CompilerParams(vmem_limit_bytes=mib * 2**20)


def cost(flops, moved):
    return pl.CostEstimate(flops=int(flops), bytes_accessed=int(moved), transcendentals=0)


def sds(shape, dtype):
    return jax.ShapeDtypeStruct(shape, dtype)


def pack(owners, local, ids, gate, hidden):
    routes, width = hidden.shape
    return pl.pallas_call(
        functools.partial(pack_kernel, owners, local),
        out_shape=[sds((owners, local * CAP + EXTRA, width), BF16), sds(ids.shape, F32)],
        in_specs=[VMEM] * 3,
        out_specs=[VMEM] * 2,
        compiler_params=params(20),
        cost_estimate=cost(2 * owners * local * CAP * routes * width, 2**22),
        name="pack",
    )(ids, gate, hidden)


def expert_call(local, at, wire, grads, pieces):
    owners, tokens, model = grads.shape
    width = wire.shape[2]
    depth = model // (SIDE * SIDE)
    rows = owners * CAP
    return pl.pallas_call(
        functools.partial(expert_kernel, local),
        out_shape=[sds((SIDE, local // 2, width, depth), BF16)] * (2 * SIDE)
        + [sds((owners, local * CAP, width), BF16)],
        in_specs=[SMEM, VMEM] + [HBM] * (1 + len(pieces)),
        out_specs=[HBM] * (2 * SIDE + 1),
        scratch_shapes=[
            pltpu.VMEM((owners, tokens, model), BF16),
            pltpu.VMEM((local, rows, model), BF16),
            pltpu.VMEM((2, SIDE, SIDE, local // 2, width, depth), BF16),
            pltpu.VMEM((2, SIDE, SIDE, local // 2, depth, width), BF16),
            pltpu.VMEM((owners, local * CAP, width), F32),
            pltpu.VMEM((owners, local * CAP, width), BF16),
            pltpu.SemaphoreType.DMA((owners // 2,)),
            pltpu.SemaphoreType.DMA((2, SIDE)),
            pltpu.SemaphoreType.DMA((2, SIDE)),
            pltpu.SemaphoreType.DMA,
        ],
        compiler_params=params(40),
        cost_estimate=cost(6.4e9, 24e6),
        name="experts",
    )(at, wire, grads, *pieces)


def unpack(ids, pos, gate, hidden, back):
    routes, width = hidden.shape
    return pl.pallas_call(
        unpack_kernel,
        out_shape=[sds((routes, width), BF16), sds(ids.shape, BF16)],
        in_specs=[VMEM] * 5,
        out_specs=[VMEM] * 2,
        compiler_params=params(20),
        cost_estimate=cost(2 * back.shape[0] * routes * width, 2**22),
        name="unpack",
    )(ids, pos, gate, hidden, back)


def finish(parts, depth, local, width):
    return pl.pallas_call(
        finish_kernel,
        out_shape=sds((depth, local, width), F32),
        in_specs=[VMEM] * len(parts),
        out_specs=VMEM,
        compiler_params=params(12),
        cost_estimate=cost(2**20, 2.5e6),
        name="finish",
    )(*parts)


def per_device(out_grad, saved_hidden, gate_weight, expert_ids, down_weight):
    tokens, top = expert_ids.shape
    width = saved_hidden.shape[2]
    owners = lax.axis_size("expert")
    depth, local, _ = down_weight.shape
    dp = lax.axis_index("dp").astype(I32)
    at = jnp.stack([dp // SIDE, dp % SIDE])
    half = local // 2

    grads = lax.all_gather(out_grad, "expert", axis=0, tiled=False)
    ids, gate = expert_ids.T, gate_weight.T
    hidden = saved_hidden.reshape(tokens * top, width)
    wire, pos = pack(owners, local, ids, gate, hidden)
    wire = lax.all_to_all(wire, "expert", split_axis=0, concat_axis=0, tiled=True)
    weights = down_weight.transpose(1, 0, 2)
    pieces = gather_half(weights[:half], 0) + gather_half(weights[half:], 1)

    *messages, u = expert_call(local, at, wire, grads, pieces)
    back = lax.all_to_all(u, "expert", split_axis=0, concat_axis=0, tiled=True)
    sums = scatter_half(messages[:SIDE], 0) + scatter_half(messages[SIDE:], 1)
    back = back.reshape(owners * local * CAP, width)
    grad_hidden, grad_gate = unpack(ids, pos, gate, hidden, back)
    grad_down = finish(sums, depth, local, width)
    return grad_hidden.reshape(tokens, top, width), grad_gate.T, grad_down


def solution(mesh):
    in_specs = (
        P(("dp", "expert"), None),
        P(("dp", "expert"), None, None),
        P(("dp", "expert"), None),
        P(("dp", "expert"), None),
        P("dp", "expert", None),
    )
    out_specs = (
        P(("dp", "expert"), None, None),
        P(("dp", "expert"), None),
        P("dp", "expert", None),
    )
    return jax.shard_map(
        per_device, mesh=mesh, in_specs=in_specs, out_specs=out_specs, check_vma=False
    )
```

profile of v0, /device:TPU:6, one launch (start us, length us, event | category | flops | bytes accessed | tf_op | source)
XLA Modules:
  0.0 199.9 jit_solution(15981537922025659127)
XLA Ops:
  7.9 1.1 copy-done
  10.4 3.2 %pack.1 = (bf16[16,104,384]{2,1,0:T(8,128)(2,1)}, f32[8,128]{1,0:T(8,128)S(1)}) custom-call(s32[8,128]{1,0:T(8,128)S(1)} %bitcast.41, bf16[8,128]{1,0:T(8,128)(2,1)S(1)} %bitcast.43, bf16[1024,384]{1,0:T(8,128)(2,1)S(1)} %bitcast.39), custom_call_target="tpu_custom_call" | custom-call | flops 1207959552 | bytes 4194304 | tf_op jit(solution)/shard_map/pack/pallas_call | solution.py:228
  13.6 8.8 %all-to-all-start = ((bf16[16,104,384]{2,1,0:T(8,128)(2,1)}), bf16[16,104,384]{2,1,0:T(8,128)(2,1)}, u32[]{:S(2)}, u32[]{:S(2)}) async-start(bf16[16,104,384]{2,1,0:T(8,128)(2,1)} %get-tuple-element.17), calls=%async_computation | async-start | bytes 2555904 | tf_op jit(solution)/shard_map/all_to_all | solution.py:306
  22.5 1.5 collective-permute-start.1
  24.0 3.2 %collective-permute-start.2 = (bf16[2,128,384]{2,1,0:T(8,128)(2,1)S(1)}, bf16[2,128,384]{2,1,0:T(8,128)(2,1)S(1)}, u32[]{:S(2)}, u32[]{:S(2)}) collective-permute-start(bf16[2,128,384]{2,1,0:T(8,128)(2,1)S(1)} %get-tuple-element.40), channel_id=1, source_target_pairs={{0,64},{16,80},{32,96},{48,112},{64,128},{80,144},{96,160},{112,17... | collective-permute-start | bytes 589832 | tf_op jit(solution)/shard_map/ppermute | solution.py:190
  27.2 4.6 %collective-permute-done.1 = bf16[2,128,384]{2,1,0:T(8,128)(2,1)S(1)} collective-permute-done((bf16[2,128,384]{2,1,0:T(8,128)(2,1)S(1)}, bf16[2,128,384]{2,1,0:T(8,128)(2,1)S(1)}, u32[]{:S(2)}, u32[]{:S(2)}) %collective-permute-start.1) | collective-permute-done | bytes 196640 | tf_op jit(solution)/shard_map/ppermute | solution.py:190
  31.8 3.6 %collective-permute-done = bf16[2,128,384]{2,1,0:T(8,128)(2,1)S(1)} collective-permute-done((bf16[2,128,384]{2,1,0:T(8,128)(2,1)S(1)}, bf16[2,128,384]{2,1,0:T(8,128)(2,1)S(1)}, u32[]{:S(2)}, u32[]{:S(2)}) %collective-permute-start) | collective-permute-done | bytes 196640 | tf_op jit(solution)/shard_map/ppermute | solution.py:190
  35.6 1.6 collective-permute-start.5
  37.2 2.9 %collective-permute-start.7 = (bf16[2,128,384]{2,1,0:T(8,128)(2,1)S(1)}, bf16[2,128,384]{2,1,0:T(8,128)(2,1)S(1)}, u32[]{:S(2)}, u32[]{:S(2)}) collective-permute-start(bf16[2,128,384]{2,1,0:T(8,128)(2,1)S(1)} %get-tuple-element.39), channel_id=1, source_target_pairs={{0,32},{16,48},{32,0},{48,16},{64,96},{80,112},{96,64},{112,80},{1... | collective-permute-start | bytes 589832 | tf_op jit(solution)/shard_map/ppermute | solution.py:190
  40.1 1.3 collective-permute-start.6
  42.2 0.8 collective-permute-start.4
  42.9 19.8 %collective-permute-done.7 = bf16[2,128,384]{2,1,0:T(8,128)(2,1)S(1)} collective-permute-done((bf16[2,128,384]{2,1,0:T(8,128)(2,1)S(1)}, bf16[2,128,384]{2,1,0:T(8,128)(2,1)S(1)}, u32[]{:S(2)}, u32[]{:S(2)}) %collective-permute-start.7) | collective-permute-done | bytes 196640 | tf_op jit(solution)/shard_map/ppermute | solution.py:190
  62.8 2.2 %collective-permute-done.8 = bf16[2,128,384]{2,1,0:T(8,128)(2,1)S(1)} collective-permute-done((bf16[2,128,384]{2,1,0:T(8,128)(2,1)S(1)}, bf16[2,128,384]{2,1,0:T(8,128)(2,1)S(1)}, u32[]{:S(2)}, u32[]{:S(2)}) %collective-permute-start.8) | collective-permute-done | bytes 196640 | tf_op jit(solution)/shard_map/ppermute | solution.py:190
  65.4 2.6 %collective-permute-start.10 = (bf16[4,2,128,384]{3,2,1,0:T(8,128)(2,1)S(1)}, bf16[4,2,128,384]{3,2,1,0:T(8,128)(2,1)}, u32[]{:S(2)}, u32[]{:S(2)}) collective-permute-start(bf16[4,2,128,384]{3,2,1,0:T(8,128)(2,1)S(1)} %pad_maximum_fusion.1.refs_4_), channel_id=1, source_target_pairs={{0,128},{16,144},{32,160},{48,176},{64,192},{80,208},{96,224},{112... | collective-permute-start | bytes 2359304 | tf_op jit(solution)/shard_map/ppermute | solution.py:190
  68.0 0.9 copy-done.2
  69.0 14.0 %collective-permute-done.4.refs_2_ = bf16[4,2,128,384]{3,2,1,0:T(8,128)(2,1)S(1)} collective-permute-done((bf16[4,2,128,384]{3,2,1,0:T(8,128)(2,1)S(1)}, bf16[4,2,128,384]{3,2,1,0:T(8,128)(2,1)S(1)}, u32[]{:S(2)}, u32[]{:S(2)}) %collective-permute-start.4) | collective-permute-done | bytes 786464 | tf_op jit(solution)/shard_map/ppermute | solution.py:190
  83.0 0.9 copy-done.4
  83.9 0.9 copy-done.6
  84.8 0.9 collective-permute-done.11.refs_7_
  85.7 1.8 collective-permute-done.10.refs_6_
  87.5 15.1 %collective-permute-done.9.refs_5_ = bf16[4,2,128,384]{3,2,1,0:T(8,128)(2,1)} collective-permute-done((bf16[4,2,128,384]{3,2,1,0:T(8,128)(2,1)S(1)}, bf16[4,2,128,384]{3,2,1,0:T(8,128)(2,1)}, u32[]{:S(2)}, u32[]{:S(2)}) %collective-permute-start.9) | collective-permute-done | bytes 786464 | tf_op jit(solution)/shard_map/ppermute | solution.py:190
  102.6 1.1 copy-done.3
  103.8 1.1 copy-done.5
  104.9 1.1 copy-done.7
  106.0 14.9 %experts.1 = (bf16[4,2,384,128]{3,2,1,0:T(8,128)(2,1)S(1)}, bf16[4,2,384,128]{3,2,1,0:T(8,128)(2,1)S(1)}, bf16[4,2,384,128]{3,2,1,0:T(8,128)(2,1)S(1)}, bf16[4,2...) custom-call(s32[2]{0:T(128)S(1)} %pad_add_fusion.at_ref, ...), custom_call_target="tpu_custom_call" | custom-call | flops 6400000000 | bytes 24000000 | tf_op jit(solution)/shard_map/experts/pallas_call | solution.py:244
  121.0 0.9 copy-done.8
  121.9 0.9 copy-done.9
  122.7 0.9 copy-done.10
  123.6 0.9 copy-done.11
  124.5 0.9 copy-done.12
  125.4 0.9 copy-done.13
  126.3 6.9 %all-to-all-start.1 = ((bf16[16,96,384]{2,1,0:T(8,128)(2,1)}), bf16[16,96,384]{2,1,0:T(8,128)(2,1)S(1)}, u32[]{:S(2)}, u32[]{:S(2)}) async-start(bf16[16,96,384]{2,1,0:T(8,128)(2,1)} %get-tuple-element.18), calls=%async_computation.1 | async-start | bytes 2359296 | tf_op jit(solution)/shard_map/all_to_all | solution.py:311
  133.2 1.1 collective-permute-start.12
  134.4 2.0 %collective-permute-start.13 = (bf16[4,2,384,128]{3,2,1,0:T(8,128)(2,1)}, bf16[4,2,384,128]{3,2,1,0:T(8,128)(2,1)S(1)}, u32[]{:S(2)}, u32[]{:S(2)}) collective-permute-start(bf16[4,2,384,128]{3,2,1,0:T(8,128)(2,1)} %copy-done.12), channel_id=1, source_target_pairs={{0,128},{16,144},{32,160},{48,176},{64,192},{80,208},{96,224},{112... | collective-permute-start | bytes 2359304 | tf_op jit(solution)/shard_map/ppermute | solution.py:190
  136.4 0.8 collective-permute-start.14
  137.5 2.9 %collective-permute-start.19 = (bf16[4,2,384,128]{3,2,1,0:T(8,128)(2,1)}, bf16[4,2,384,128]{3,2,1,0:T(8,128)(2,1)S(1)}, u32[]{:S(2)}, u32[]{:S(2)}) collective-permute-start(bf16[4,2,384,128]{3,2,1,0:T(8,128)(2,1)} %copy-done.9), channel_id=1, source_target_pairs={{0,32},{16,48},{32,0},{48,16},{64,96},{80,112},{96,64},{112,80},{1... | collective-permute-start | bytes 2359304 | tf_op jit(solution)/shard_map/ppermute | solution.py:190
  140.4 13.5 %collective-permute-done.12 = bf16[4,2,384,128]{3,2,1,0:T(8,128)(2,1)S(1)} collective-permute-done((bf16[4,2,384,128]{3,2,1,0:T(8,128)(2,1)}, bf16[4,2,384,128]{3,2,1,0:T(8,128)(2,1)S(1)}, u32[]{:S(2)}, u32[]{:S(2)}) %collective-permute-start.12) | collective-permute-done | bytes 786464 | tf_op jit(solution)/shard_map/ppermute | solution.py:190
  153.8 1.7 collective-permute-start.20
  155.6 0.9 collective-permute-done.13
  156.5 15.9 %collective-permute-done.14 = bf16[4,2,384,128]{3,2,1,0:T(8,128)(2,1)S(1)} collective-permute-done((bf16[4,2,384,128]{3,2,1,0:T(8,128)(2,1)}, bf16[4,2,384,128]{3,2,1,0:T(8,128)(2,1)S(1)}, u32[]{:S(2)}, u32[]{:S(2)}) %collective-permute-start.14) | collective-permute-done | bytes 786464 | tf_op jit(solution)/shard_map/ppermute | solution.py:190
  172.8 1.8 collective-permute-start.17
  175.3 1.0 collective-permute-start.15
  177.3 3.9 %collective-permute-start.22 = (bf16[2,384,128]{2,1,0:T(8,128)(2,1)S(1)}, bf16[2,384,128]{2,1,0:T(8,128)(2,1)S(1)}, u32[]{:S(2)}, u32[]{:S(2)}) collective-permute-start(bf16[2,384,128]{2,1,0:T(8,128)(2,1)S(1)} %get-tuple-element.30), channel_id=1, source_target_pairs={{0,128},{16,144},{32,160},{48,176},{64,192},{80,208},{96,224},{112... | collective-permute-start | bytes 589832 | tf_op jit(solution)/shard_map/ppermute | solution.py:190
  181.2 2.2 %collective-permute-start.21 = (bf16[2,384,128]{2,1,0:T(8,128)(2,1)S(1)}, bf16[2,384,128]{2,1,0:T(8,128)(2,1)S(1)}, u32[]{:S(2)}, u32[]{:S(2)}) collective-permute-start(bf16[2,384,128]{2,1,0:T(8,128)(2,1)S(1)} %get-tuple-element.31), channel_id=1, source_target_pairs={{0,64},{16,80},{32,96},{48,112},{64,128},{80,144},{96,160},{112,17... | collective-permute-start | bytes 589832 | tf_op jit(solution)/shard_map/ppermute | solution.py:190
  184.0 2.9 %collective-permute-done.15.refs_1_ = bf16[2,384,128]{2,1,0:T(8,128)(2,1)S(1)} collective-permute-done((bf16[2,384,128]{2,1,0:T(8,128)(2,1)S(1)}, bf16[2,384,128]{2,1,0:T(8,128)(2,1)S(1)}, u32[]{:S(2)}, u32[]{:S(2)}) %collective-permute-start.15) | collective-permute-done | bytes 196640 | tf_op jit(solution)/shard_map/ppermute | solution.py:190
  186.9 1.3 collective-permute-done.23.refs_7_
  188.8 1.2 finish.1
  190.1 3.0 %unpack.1 = (bf16[1024,384]{1,0:T(8,128)(2,1)}, bf16[8,128]{1,0:T(8,128)(2,1)}) custom-call(s32[8,128]{1,0:T(8,128)S(1)} %bitcast.42, f32[8,128]{1,0:T(8,128)S(1)} %get-tuple-element.16.pos_ref, bf16[8,128]{1,0:T(8,128)(2,1)S(1)} %bitcast.44, bf16[1024,384]{1,0:T(8,128)(2,1)S(1)} %bitcast.40, bf16[1536,384]{1,0:T(8,128)(2,1)S(1)} %bitcast.38), custom_call_target="tpu_custom_call" | custom-call | flops 1207959552 | bytes 4194304 | tf_op jit(solution)/shard_map/unpack/pallas_call | solution.py:270
  (56 shorter events, 7.1 us)
Async XLA Ops:
  7.2 95.5 %all-gather.3.cloned.1.call-start = ((), (), s32[]{:S(2)}) async-start(), calls=%async_computation.2 | async-start | bytes 8912896 | tf_op jit(solution)/shard_map/all_gather | solution.py:302
  7.9 1.1 copy-start
  9.0 0.7 copy-start.14
  9.7 0.7 copy-start.16
  13.6 8.8 %copy-start.18 = (bf16[128,4,384]{2,1,0:T(4,128)(2,1)S(1)}, bf16[128,4,384]{2,1,0:T(4,128)(2,1)}, u32[]{:S(2)}) copy-start(bf16[128,4,384]{2,1,0:T(4,128)(2,1)} %param.9) | copy-start | bytes 1179652
  13.6 89.1 %all-to-all-start = ((bf16[16,104,384]{2,1,0:T(8,128)(2,1)}), bf16[16,104,384]{2,1,0:T(8,128)(2,1)}, u32[]{:S(2)}, u32[]{:S(2)}) async-start(bf16[16,104,384]{2,1,0:T(8,128)(2,1)} %get-tuple-element.17), calls=%async_computation | async-start | bytes 2555904 | tf_op jit(solution)/shard_map/all_to_all | solution.py:306
  22.5 9.4 %collective-permute-start.1 = (bf16[2,128,384]{2,1,0:T(8,128)(2,1)S(1)}, bf16[2,128,384]{2,1,0:T(8,128)(2,1)S(1)}, u32[]{:S(2)}, u32[]{:S(2)}) collective-permute-start(bf16[2,128,384]{2,1,0:T(8,128)(2,1)S(1)} %get-tuple-element.40), channel_id=1, source_target_pairs={{0,128},{16,144},{32,160},{48,176},{64,192},{80,208},{96,224},{112... | collective-permute-start | bytes 589832 | tf_op jit(solution)/shard_map/ppermute | solution.py:190
  24.0 11.5 %collective-permute-start = (bf16[2,128,384]{2,1,0:T(8,128)(2,1)S(1)}, bf16[2,128,384]{2,1,0:T(8,128)(2,1)S(1)}, u32[]{:S(2)}, u32[]{:S(2)}) collective-permute-start(bf16[2,128,384]{2,1,0:T(8,128)(2,1)S(1)} %get-tuple-element.40), channel_id=1, source_target_pairs={{0,192},{16,208},{32,224},{48,240},{64,0},{80,16},{96,32},{112,48}... | collective-permute-start | bytes 589832 | tf_op jit(solution)/shard_map/ppermute | solution.py:190
  24.0 11.5 %collective-permute-start.2 = (bf16[2,128,384]{2,1,0:T(8,128)(2,1)S(1)}, bf16[2,128,384]{2,1,0:T(8,128)(2,1)S(1)}, u32[]{:S(2)}, u32[]{:S(2)}) collective-permute-start(bf16[2,128,384]{2,1,0:T(8,128)(2,1)S(1)} %get-tuple-element.40), channel_id=1, source_target_pairs={{0,64},{16,80},{32,96},{48,112},{64,128},{80,144},{96,160},{112,17... | collective-permute-start | bytes 589832 | tf_op jit(solution)/shard_map/ppermute | solution.py:190
  35.6 32.4 %collective-permute-start.5 = (bf16[4,2,128,384]{3,2,1,0:T(8,128)(2,1)S(1)}, bf16[4,2,128,384]{3,2,1,0:T(8,128)(2,1)S(1)}, u32[]{:S(2)}, u32[]{:S(2)}) collective-permute-start(bf16[4,2,128,384]{3,2,1,0:T(8,128)(2,1)S(1)} %pad_maximum_fusion.refs_0_), channel_id=1, source_target_pairs={{0,16},{16,32},{32,48},{48,0},{64,80},{80,96},{96,112},{112,64},{1... | collective-permute-start | bytes 2359304 | tf_op jit(solution)/shard_map/ppermute | solution.py:190
  37.2 25.5 %collective-permute-start.7 = (bf16[2,128,384]{2,1,0:T(8,128)(2,1)S(1)}, bf16[2,128,384]{2,1,0:T(8,128)(2,1)S(1)}, u32[]{:S(2)}, u32[]{:S(2)}) collective-permute-start(bf16[2,128,384]{2,1,0:T(8,128)(2,1)S(1)} %get-tuple-element.39), channel_id=1, source_target_pairs={{0,32},{16,48},{32,0},{48,16},{64,96},{80,112},{96,64},{112,80},{1... | collective-permute-start | bytes 589832 | tf_op jit(solution)/shard_map/ppermute | solution.py:190
  40.1 22.6 %collective-permute-start.6 = (bf16[2,128,384]{2,1,0:T(8,128)(2,1)S(1)}, bf16[2,128,384]{2,1,0:T(8,128)(2,1)S(1)}, u32[]{:S(2)}, u32[]{:S(2)}) collective-permute-start(bf16[2,128,384]{2,1,0:T(8,128)(2,1)S(1)} %get-tuple-element.39), channel_id=1, source_target_pairs={{0,48},{16,0},{32,16},{48,32},{64,112},{80,64},{96,80},{112,96},{1... | collective-permute-start | bytes 589832 | tf_op jit(solution)/shard_map/ppermute | solution.py:190
  41.5 23.5 %collective-permute-start.8 = (bf16[2,128,384]{2,1,0:T(8,128)(2,1)S(1)}, bf16[2,128,384]{2,1,0:T(8,128)(2,1)S(1)}, u32[]{:S(2)}, u32[]{:S(2)}) collective-permute-start(bf16[2,128,384]{2,1,0:T(8,128)(2,1)S(1)} %get-tuple-element.39), channel_id=1, source_target_pairs={{0,16},{16,32},{32,48},{48,0},{64,80},{80,96},{96,112},{112,64},{1... | collective-permute-start | bytes 589832 | tf_op jit(solution)/shard_map/ppermute | solution.py:190
  42.2 40.9 %collective-permute-start.4 = (bf16[4,2,128,384]{3,2,1,0:T(8,128)(2,1)S(1)}, bf16[4,2,128,384]{3,2,1,0:T(8,128)(2,1)S(1)}, u32[]{:S(2)}, u32[]{:S(2)}) collective-permute-start(bf16[4,2,128,384]{3,2,1,0:T(8,128)(2,1)S(1)} %pad_maximum_fusion.refs_0_), channel_id=1, source_target_pairs={{0,32},{16,48},{32,0},{48,16},{64,96},{80,112},{96,64},{112,80},{1... | collective-permute-start | bytes 2359304 | tf_op jit(solution)/shard_map/ppermute | solution.py:190
  62.8 21.1 %collective-permute-start.3 = (bf16[4,2,128,384]{3,2,1,0:T(8,128)(2,1)S(1)}, bf16[4,2,128,384]{3,2,1,0:T(8,128)(2,1)S(1)}, u32[]{:S(2)}, u32[]{:S(2)}) collective-permute-start(bf16[4,2,128,384]{3,2,1,0:T(8,128)(2,1)S(1)} %pad_maximum_fusion.refs_0_), channel_id=1, source_target_pairs={{0,48},{16,0},{32,16},{48,32},{64,112},{80,64},{96,80},{112,96},{1... | collective-permute-start | bytes 2359304 | tf_op jit(solution)/shard_map/ppermute | solution.py:190
  65.1 20.7 %collective-permute-start.11 = (bf16[4,2,128,384]{3,2,1,0:T(8,128)(2,1)S(1)}, bf16[4,2,128,384]{3,2,1,0:T(8,128)(2,1)}, u32[]{:S(2)}, u32[]{:S(2)}) collective-permute-start(bf16[4,2,128,384]{3,2,1,0:T(8,128)(2,1)S(1)} %pad_maximum_fusion.1.refs_4_), channel_id=1, source_target_pairs={{0,64},{16,80},{32,96},{48,112},{64,128},{80,144},{96,160},{112,17... | collective-permute-start | bytes 2359304 | tf_op jit(solution)/shard_map/ppermute | solution.py:190
  65.4 22.1 %collective-permute-start.10 = (bf16[4,2,128,384]{3,2,1,0:T(8,128)(2,1)S(1)}, bf16[4,2,128,384]{3,2,1,0:T(8,128)(2,1)}, u32[]{:S(2)}, u32[]{:S(2)}) collective-permute-start(bf16[4,2,128,384]{3,2,1,0:T(8,128)(2,1)S(1)} %pad_maximum_fusion.1.refs_4_), channel_id=1, source_target_pairs={{0,128},{16,144},{32,160},{48,176},{64,192},{80,208},{96,224},{112... | collective-permute-start | bytes 2359304 | tf_op jit(solution)/shard_map/ppermute | solution.py:190
  68.0 0.9 copy-start.2
  68.9 33.7 %collective-permute-start.9 = (bf16[4,2,128,384]{3,2,1,0:T(8,128)(2,1)S(1)}, bf16[4,2,128,384]{3,2,1,0:T(8,128)(2,1)}, u32[]{:S(2)}, u32[]{:S(2)}) collective-permute-start(bf16[4,2,128,384]{3,2,1,0:T(8,128)(2,1)S(1)} %pad_maximum_fusion.1.refs_4_), channel_id=1, source_target_pairs={{0,192},{16,208},{32,224},{48,240},{64,0},{80,16},{96,32},{112,48}... | collective-permute-start | bytes 2359304 | tf_op jit(solution)/shard_map/ppermute | solution.py:190
  83.0 0.9 copy-start.4
  83.9 0.9 copy-start.6
  102.6 1.1 copy-start.3
  103.8 1.1 copy-start.5
  104.9 1.1 copy-start.7
  120.9 0.9 copy-start.8
  121.9 0.9 copy-start.9
  122.7 0.9 copy-start.10
  123.6 0.9 copy-start.11
  124.5 0.9 copy-start.12
  125.4 0.9 copy-start.13
  126.3 63.8 %all-to-all-start.1 = ((bf16[16,96,384]{2,1,0:T(8,128)(2,1)}), bf16[16,96,384]{2,1,0:T(8,128)(2,1)S(1)}, u32[]{:S(2)}, u32[]{:S(2)}) async-start(bf16[16,96,384]{2,1,0:T(8,128)(2,1)} %get-tuple-element.18), calls=%async_computation.1 | async-start | bytes 2359296 | tf_op jit(solution)/shard_map/all_to_all | solution.py:311
  133.2 20.6 %collective-permute-start.12 = (bf16[4,2,384,128]{3,2,1,0:T(8,128)(2,1)}, bf16[4,2,384,128]{3,2,1,0:T(8,128)(2,1)S(1)}, u32[]{:S(2)}, u32[]{:S(2)}) collective-permute-start(bf16[4,2,384,128]{3,2,1,0:T(8,128)(2,1)} %copy-done.13), channel_id=1, source_target_pairs={{0,64},{16,80},{32,96},{48,112},{64,128},{80,144},{96,160},{112,17... | collective-permute-start | bytes 2359304 | tf_op jit(solution)/shard_map/ppermute | solution.py:190
  134.4 22.2 %collective-permute-start.13 = (bf16[4,2,384,128]{3,2,1,0:T(8,128)(2,1)}, bf16[4,2,384,128]{3,2,1,0:T(8,128)(2,1)S(1)}, u32[]{:S(2)}, u32[]{:S(2)}) collective-permute-start(bf16[4,2,384,128]{3,2,1,0:T(8,128)(2,1)} %copy-done.12), channel_id=1, source_target_pairs={{0,128},{16,144},{32,160},{48,176},{64,192},{80,208},{96,224},{112... | collective-permute-start | bytes 2359304 | tf_op jit(solution)/shard_map/ppermute | solution.py:190
  136.4 36.0 %collective-permute-start.14 = (bf16[4,2,384,128]{3,2,1,0:T(8,128)(2,1)}, bf16[4,2,384,128]{3,2,1,0:T(8,128)(2,1)S(1)}, u32[]{:S(2)}, u32[]{:S(2)}) collective-permute-start(bf16[4,2,384,128]{3,2,1,0:T(8,128)(2,1)} %copy-done.11), channel_id=1, source_target_pairs={{0,192},{16,208},{32,224},{48,240},{64,0},{80,16},{96,32},{112,48}... | collective-permute-start | bytes 2359304 | tf_op jit(solution)/shard_map/ppermute | solution.py:190
  137.2 38.1 %collective-permute-start.18 = (bf16[4,2,384,128]{3,2,1,0:T(8,128)(2,1)}, bf16[4,2,384,128]{3,2,1,0:T(8,128)(2,1)S(1)}, u32[]{:S(2)}, u32[]{:S(2)}) collective-permute-start(bf16[4,2,384,128]{3,2,1,0:T(8,128)(2,1)} %copy-done.10), channel_id=1, source_target_pairs={{0,16},{16,32},{32,48},{48,0},{64,80},{80,96},{96,112},{112,64},{1... | collective-permute-start | bytes 2359304 | tf_op jit(solution)/shard_map/ppermute | solution.py:190
  137.5 38.8 %collective-permute-start.19 = (bf16[4,2,384,128]{3,2,1,0:T(8,128)(2,1)}, bf16[4,2,384,128]{3,2,1,0:T(8,128)(2,1)S(1)}, u32[]{:S(2)}, u32[]{:S(2)}) collective-permute-start(bf16[4,2,384,128]{3,2,1,0:T(8,128)(2,1)} %copy-done.9), channel_id=1, source_target_pairs={{0,32},{16,48},{32,0},{48,16},{64,96},{80,112},{96,64},{112,80},{1... | collective-permute-start | bytes 2359304 | tf_op jit(solution)/shard_map/ppermute | solution.py:190
  153.8 22.4 %collective-permute-start.20 = (bf16[4,2,384,128]{3,2,1,0:T(8,128)(2,1)}, bf16[4,2,384,128]{3,2,1,0:T(8,128)(2,1)S(1)}, u32[]{:S(2)}, u32[]{:S(2)}) collective-permute-start(bf16[4,2,384,128]{3,2,1,0:T(8,128)(2,1)} %copy-done.8), channel_id=1, source_target_pairs={{0,48},{16,0},{32,16},{48,32},{64,112},{80,64},{96,80},{112,96},{1... | collective-permute-start | bytes 2359304 | tf_op jit(solution)/shard_map/ppermute | solution.py:190
  172.8 8.4 %collective-permute-start.17 = (bf16[2,384,128]{2,1,0:T(8,128)(2,1)S(1)}, bf16[2,384,128]{2,1,0:T(8,128)(2,1)S(1)}, u32[]{:S(2)}, u32[]{:S(2)}) collective-permute-start(bf16[2,384,128]{2,1,0:T(8,128)(2,1)S(1)} %get-tuple-element.33), channel_id=1, source_target_pairs={{0,48},{16,0},{32,16},{48,32},{64,112},{80,64},{96,80},{112,96},{1... | collective-permute-start | bytes 589832 | tf_op jit(solution)/shard_map/ppermute | solution.py:190
  174.6 9.4 %collective-permute-start.16 = (bf16[2,384,128]{2,1,0:T(8,128)(2,1)S(1)}, bf16[2,384,128]{2,1,0:T(8,128)(2,1)S(1)}, u32[]{:S(2)}, u32[]{:S(2)}) collective-permute-start(bf16[2,384,128]{2,1,0:T(8,128)(2,1)S(1)} %get-tuple-element.34), channel_id=1, source_target_pairs={{0,32},{16,48},{32,0},{48,16},{64,96},{80,112},{96,64},{112,80},{1... | collective-permute-start | bytes 589832 | tf_op jit(solution)/shard_map/ppermute | solution.py:190
  175.3 11.6 %collective-permute-start.15 = (bf16[2,384,128]{2,1,0:T(8,128)(2,1)S(1)}, bf16[2,384,128]{2,1,0:T(8,128)(2,1)S(1)}, u32[]{:S(2)}, u32[]{:S(2)}) collective-permute-start(bf16[2,384,128]{2,1,0:T(8,128)(2,1)S(1)} %get-tuple-element.35), channel_id=1, source_target_pairs={{0,16},{16,32},{32,48},{48,0},{64,80},{80,96},{96,112},{112,64},{1... | collective-permute-start | bytes 589832 | tf_op jit(solution)/shard_map/ppermute | solution.py:190
  176.7 13.3 %copy-start.1 = (bf16[128,8,384]{2,1,0:T(8,128)(2,1)S(1)}, bf16[128,8,384]{2,1,0:T(8,128)(2,1)}, u32[]{:S(2)}) copy-start(bf16[128,8,384]{2,1,0:T(8,128)(2,1)} %param.6) | copy-start | bytes 2359300
  176.7 13.3 %copy-start.15 = (s32[128,8]{0,1:T(8,128)S(1)}, s32[128,8]{0,1:T(8,128)}, u32[]{:S(2)}) copy-start(s32[128,8]{0,1:T(8,128)} %param.8) | copy-start | bytes 12292
  176.7 13.3 %copy-start.17 = (bf16[128,8]{0,1:T(8,128)(2,1)S(1)}, bf16[128,8]{0,1:T(8,128)(2,1)}, u32[]{:S(2)}) copy-start(bf16[128,8]{0,1:T(8,128)(2,1)} %param.7) | copy-start | bytes 6148
  176.7 11.5 %collective-permute-start.23 = (bf16[2,384,128]{2,1,0:T(8,128)(2,1)S(1)}, bf16[2,384,128]{2,1,0:T(8,128)(2,1)S(1)}, u32[]{:S(2)}, u32[]{:S(2)}) collective-permute-start(bf16[2,384,128]{2,1,0:T(8,128)(2,1)S(1)} %get-tuple-element.29), channel_id=1, source_target_pairs={{0,192},{16,208},{32,224},{48,240},{64,0},{80,16},{96,32},{112,48}... | collective-permute-start | bytes 589832 | tf_op jit(solution)/shard_map/ppermute | solution.py:190
  177.3 10.9 %collective-permute-start.22 = (bf16[2,384,128]{2,1,0:T(8,128)(2,1)S(1)}, bf16[2,384,128]{2,1,0:T(8,128)(2,1)S(1)}, u32[]{:S(2)}, u32[]{:S(2)}) collective-permute-start(bf16[2,384,128]{2,1,0:T(8,128)(2,1)S(1)} %get-tuple-element.30), channel_id=1, source_target_pairs={{0,128},{16,144},{32,160},{48,176},{64,192},{80,208},{96,224},{112... | collective-permute-start | bytes 589832 | tf_op jit(solution)/shard_map/ppermute | solution.py:190
  181.2 7.6 %collective-permute-start.21 = (bf16[2,384,128]{2,1,0:T(8,128)(2,1)S(1)}, bf16[2,384,128]{2,1,0:T(8,128)(2,1)S(1)}, u32[]{:S(2)}, u32[]{:S(2)}) collective-permute-start(bf16[2,384,128]{2,1,0:T(8,128)(2,1)S(1)} %get-tuple-element.31), channel_id=1, source_target_pairs={{0,64},{16,80},{32,96},{48,112},{64,128},{80,144},{96,160},{112,17... | collective-permute-start | bytes 589832 | tf_op jit(solution)/shard_map/ppermute | solution.py:190
Sparse Core Ops, SparseCore 0:
  9.8 85.1 all-gather.2
where the time goes:
time: 204 us; the launch traced here: 200 us
  waiting for transfers between devices  98.5 us (48%)
  starting transfers between devices  49.8 us (24%)
  Pallas kernels  22.3 us (11%)
  between operations  14.2 us (7%)
  local copies, waits for them, and re-layouts  14 us (7%)
    ppermute x24, waiting for transfers between devices, shift(): return lax.ppermute(x, 'dp', pairs)  97.8 us
    ppermute x24, starting transfers between devices, shift(): return lax.ppermute(x, 'dp', pairs)  34.1 us
    pallas_call x1, Pallas kernels, expert_call(): pl.pallas_call(functools.partial(expert_kernel, local), out_shape=[sds((S...  14.9 us
    unnamed x39, local copies, waits for them, and re-layouts  13.9 us
    all_to_all x1, starting transfers between devices, per_device(): lax.all_to_all(wire, 'expert', split_axis=0, concat_axis=0, tiled=True)  8.75 us
    all_to_all x1, starting transfers between devices, per_device(): back = lax.all_to_all(u, 'expert', split_axis=0, concat_axis=0, tiled=True)  6.93 us
  transfers between devices with their start and end apart: 27, of which 15 were waited for; matrix products, arithmetic and copies ran while one was open for 1% of the time, Pallas kernels for 2%

commit v1 on v0

--- a/solution.py
+++ b/solution.py
@@ -76,7 +76,14 @@
         for p in range(chips)
     ]
     weights = [
-        [pltpu.make_async_copy(pieces[h * SIDE + a], wbuf.at[h, a], wsem.at[h, a]) for a in range(SIDE)]
+        [
+            pltpu.make_async_copy(
+                pieces[h * SIDE + k],
+                wbuf.at[h, at_ref[2] * k + (1 - at_ref[2]) * ((SIDE - k) % SIDE)],
+                wsem.at[h, k],
+            )
+            for k in range(SIDE)
+        ]
         for h in range(2)
     ]
     for c in loads + weights[0] + weights[1]:
@@ -171,7 +178,7 @@
     ).astype(BF16)
 
 
-def finish_kernel(*refs):
+def finish_kernel(after_ref, *refs):
     out_ref = refs[-1]
     half = out_ref.shape[1] // 2
     for h in range(2):
@@ -181,18 +188,22 @@
             out_ref[:, h * half + e, :] = total.T
 
 
-def shift(x, axis, step):
+def shift(x, axis, step, by_core=False):
+    owners = lax.axis_size("expert")
     pairs = []
-    for i in range(SIDE):
-        for j in range(SIDE):
-            to = ((i + step) % SIDE, j) if axis == 0 else (i, (j + step) % SIDE)
-            pairs.append((i * SIDE + j, to[0] * SIDE + to[1]))
-    return lax.ppermute(x, "dp", pairs)
+    for n in range(SIDE * SIDE * owners):
+        i, j, k = n // owners // SIDE, n // owners % SIDE, n % owners
+        by = -step if by_core and k % 2 else step
+        i, j = ((i + by) % SIDE, j) if axis == 0 else (i, (j + by) % SIDE)
+        pairs.append((n, (i * SIDE + j) * owners + k))
+    return lax.ppermute(x, ("dp", "expert"), pairs)
 
 
 def gather_half(weights, first):
-    blocks = jnp.stack([weights] + [shift(weights, first, -d) for d in range(1, SIDE)])
-    return [blocks] + [shift(blocks, 1 - first, -d) for d in range(1, SIDE)]
+    blocks = [jnp.stack([weights] + [shift(weights, first, -d) for d in range(1, SIDE)])]
+    for _ in range(1, SIDE):
+        blocks.append(shift(blocks[-1], 1 - first, 1, by_core=True))
+    return [pltpu.with_memory_space_constraint(b, pltpu.HBM) for b in blocks]
 
 
 def add(*parts):
@@ -243,8 +254,8 @@
     rows = owners * CAP
     return pl.pallas_call(
         functools.partial(expert_kernel, local),
-        out_shape=[sds((SIDE, local // 2, width, depth), BF16)] * (2 * SIDE)
-        + [sds((owners, local * CAP, width), BF16)],
+        out_shape=[pltpu.HBM((SIDE, local // 2, width, depth), BF16)] * (2 * SIDE)
+        + [pltpu.HBM((owners, local * CAP, width), BF16)],
         in_specs=[SMEM, VMEM] + [HBM] * (1 + len(pieces)),
         out_specs=[HBM] * (2 * SIDE + 1),
         scratch_shapes=[
@@ -262,7 +273,7 @@
         compiler_params=params(40),
         cost_estimate=cost(6.4e9, 24e6),
         name="experts",
-    )(at, wire, grads, *pieces)
+    )(at, wire, pltpu.with_memory_space_constraint(grads, pltpu.HBM), *pieces)
 
 
 def unpack(ids, pos, gate, hidden, back):
@@ -278,16 +289,16 @@
     )(ids, pos, gate, hidden, back)
 
 
-def finish(parts, depth, local, width):
+def finish(parts, after, depth, local, width):
     return pl.pallas_call(
         finish_kernel,
         out_shape=sds((depth, local, width), F32),
-        in_specs=[VMEM] * len(parts),
+        in_specs=[ANY] + [VMEM] * len(parts),
         out_specs=VMEM,
         compiler_params=params(12),
         cost_estimate=cost(2**20, 2.5e6),
         name="finish",
-    )(*parts)
+    )(after, *parts)
 
 
 def per_device(out_grad, saved_hidden, gate_weight, expert_ids, down_weight):
@@ -296,7 +307,7 @@
     owners = lax.axis_size("expert")
     depth, local, _ = down_weight.shape
     dp = lax.axis_index("dp").astype(I32)
-    at = jnp.stack([dp // SIDE, dp % SIDE])
+    at = jnp.stack([dp // SIDE, dp % SIDE, lax.axis_index("expert").astype(I32) % 2])
     half = local // 2
 
     grads = lax.all_gather(out_grad, "expert", axis=0, tiled=False)
@@ -312,7 +323,7 @@
     sums = scatter_half(messages[:SIDE], 0) + scatter_half(messages[SIDE:], 1)
     back = back.reshape(owners * local * CAP, width)
     grad_hidden, grad_gate = unpack(ids, pos, gate, hidden, back)
-    grad_down = finish(sums, depth, local, width)
+    grad_down = finish(sums, grad_gate, depth, local, width)
     return grad_hidden.reshape(tokens, top, width), grad_gate.T, grad_down
 
 

time: 204 us -> 184 us (0.902)
  local copies, waits for them, and re-layouts: 14 us -> 2.55 us
  waiting for transfers between devices: 98.5 us -> 90.3 us
  other arithmetic: 1.14 us -> 4.96 us
  starting transfers between devices: 49.8 us -> 47.5 us
    ppermute x24, waiting for transfers between devices: 97.8 us -> 57.5 us  [shift(): return lax.ppermute(x, ('dp', 'expert'), pairs)]
    all_gather x1, waiting for transfers between devices: 0.01 us -> 20.1 us  [per_device(): grads = lax.all_gather(out_grad, 'expert', axis=0, tiled=False)]
    all_to_all x1, waiting for transfers between devices: 0.01 us -> 12.1 us  [per_device(): lax.all_to_all(wire, 'expert', split_axis=0, concat_axis=0, tiled=True)]
    unnamed x39 -> x27, local copies, waits for them, and re-layouts: 13.9 us -> 2.48 us
    all_to_all x1, starting transfers between devices: 6.93 us -> 4.53 us  [per_device(): back = lax.all_to_all(u, 'expert', split_axis=0, concat_axis=0, tiled=True)]
    another operation x2, other arithmetic: 0.25 us -> 2.55 us  [gather_half(): jnp.stack([weights] + [shift(weights, first, -d) for d in range(1, SIDE)])]
  transfers between devices with their start and end apart: 27 -> 27, of which waited for: 15 -> 13; matrix products, arithmetic and copies ran while one was open for 1% -> 3% of each run, Pallas kernels for 2% -> 3%
where the time goes in v1:
time: 184 us; the launch traced here: 181 us
  waiting for transfers between devices  90.3 us (49%)
  starting transfers between devices  47.5 us (26%)
  Pallas kernels  21.8 us (12%)
  between operations  14.2 us (8%)
  other arithmetic  4.96 us (3%)
  local copies, waits for them, and re-layouts  2.55 us (1%)
    ppermute x24, waiting for transfers between devices, shift(): return lax.ppermute(x, ('dp', 'expert'), pairs)  57.5 us
    ppermute x24, starting transfers between devices, shift(): return lax.ppermute(x, ('dp', 'expert'), pairs)  34.4 us
    all_gather x1, waiting for transfers between devices, per_device(): grads = lax.all_gather(out_grad, 'expert', axis=0, tiled=False)  20.1 us
    pallas_call x1, Pallas kernels, expert_call(): pl.pallas_call(functools.partial(expert_kernel, local), out_shape=[pltpu....  14.2 us
    all_to_all x1, waiting for transfers between devices, per_device(): lax.all_to_all(wire, 'expert', split_axis=0, concat_axis=0, tiled=True)  12.1 us
    all_to_all x1, starting transfers between devices, per_device(): lax.all_to_all(wire, 'expert', split_axis=0, concat_axis=0, tiled=True)  8.57 us
    all_to_all x1, starting transfers between devices, per_device(): back = lax.all_to_all(u, 'expert', split_axis=0, concat_axis=0, tiled=True)  4.53 us
  transfers between devices with their start and end apart: 27, of which 13 were waited for; matrix products, arithmetic and copies ran while one was open for 3% of the time, Pallas kernels for 3%

profile of v1, /device:TPU:6, one launch (start us, length us, event | category | flops | bytes accessed | tf_op | source)
XLA Modules:
  0.0 181.4 jit_solution(11831287528299301665)
XLA Ops:
  7.2 0.7 all-gather.3.cloned.1.call-update
  7.9 1.0 copy.10
  9.1 1.5 collective-permute-start.1
  10.5 1.7 collective-permute-start
  12.2 1.6 collective-permute-start.2
  13.8 3.2 %collective-permute-start.7 = (bf16[2,128,384]{2,1,0:T(8,128)(2,1)S(1)}, bf16[2,128,384]{2,1,0:T(8,128)(2,1)}, u32[]{:S(2)}, u32[]{:S(2)}) collective-permute-start(bf16[2,128,384]{2,1,0:T(8,128)(2,1)S(1)} %get-tuple-element.39), channel_id=1, source_target_pairs={{0,32},{1,33},{2,34},{3,35},{4,36},{5,37},{6,38},{7,39},{8,40},{9,... | collective-permute-start | bytes 589832 | tf_op jit(solution)/shard_map/ppermute | solution.py:199
  17.0 1.1 collective-permute-start.6
  18.0 0.4 collective-permute-done.1
  18.5 1.6 collective-permute-start.8
  20.1 3.2 %pack.1 = (bf16[16,104,384]{2,1,0:T(8,128)(2,1)}, f32[8,128]{1,0:T(8,128)S(1)}) custom-call(s32[8,128]{1,0:T(8,128)S(1)} %bitcast.43, bf16[8,128]{1,0:T(8,128)(2,1)S(1)} %bitcast.45, bf16[1024,384]{1,0:T(8,128)(2,1)S(1)} %bitcast.41), custom_call_target="tpu_custom_call" | custom-call | flops 1207959552 | bytes 4194304 | tf_op jit(solution)/shard_map/pack/pallas_call | solution.py:239
  23.2 8.6 %all-to-all-start = ((bf16[16,104,384]{2,1,0:T(8,128)(2,1)}), bf16[16,104,384]{2,1,0:T(8,128)(2,1)S(1)}, u32[]{:S(2)}, u32[]{:S(2)}) async-start(bf16[16,104,384]{2,1,0:T(8,128)(2,1)} %get-tuple-element.17), calls=%async_computation | async-start | bytes 2555904 | tf_op jit(solution)/shard_map/all_to_all | solution.py:317
  31.9 0.7 copy-done.9
  32.6 1.3 pad_maximum_fusion.refs_0_
  33.9 1.6 collective-permute-start.3
  35.5 1.3 pad_maximum_fusion.1.refs_4_
  36.8 0.6 collective-permute-start.9
  37.3 9.8 %collective-permute-done.3.refs_1_ = bf16[4,2,128,384]{3,2,1,0:T(8,128)(2,1)S(1)} collective-permute-done((bf16[4,2,128,384]{3,2,1,0:T(8,128)(2,1)S(1)}, bf16[4,2,128,384]{3,2,1,0:T(8,128)(2,1)S(1)}, u32[]{:S(2)}, u32[]{:S(2)}) %collective-permute-start.3) | collective-permute-done | bytes 786464 | tf_op jit(solution)/shard_map/ppermute | solution.py:199
  47.2 0.3 collective-permute-start.4
  47.5 1.4 collective-permute-done.9.refs_5_
  48.8 1.7 collective-permute-start.10
  50.5 9.9 %collective-permute-done.4.refs_2_ = bf16[4,2,128,384]{3,2,1,0:T(8,128)(2,1)} collective-permute-done((bf16[4,2,128,384]{3,2,1,0:T(8,128)(2,1)S(1)}, bf16[4,2,128,384]{3,2,1,0:T(8,128)(2,1)}, u32[]{:S(2)}, u32[]{:S(2)}) %collective-permute-start.4) | collective-permute-done | bytes 786464 | tf_op jit(solution)/shard_map/ppermute | solution.py:199
  60.5 0.5 collective-permute-done.10.refs_6_
  60.9 2.9 %collective-permute-start.11 = (bf16[4,2,128,384]{3,2,1,0:T(8,128)(2,1)}, bf16[4,2,128,384]{3,2,1,0:T(8,128)(2,1)}, u32[]{:S(2)}, u32[]{:S(2)}) collective-permute-start(bf16[4,2,128,384]{3,2,1,0:T(8,128)(2,1)} %collective-permute-done.10.refs_6_), channel_id=1, source_target_pairs={{0,64},{1,193},{2,66},{3,195},{4,68},{5,197},{6,70},{7,199},{8,72}... | collective-permute-start | bytes 2359304 | tf_op jit(solution)/shard_map/ppermute | solution.py:199
  63.9 12.1 %all-to-all-done.wire_ref = bf16[16,104,384]{2,1,0:T(8,128)(2,1)S(1)} async-done(((bf16[16,104,384]{2,1,0:T(8,128)(2,1)}), bf16[16,104,384]{2,1,0:T(8,128)(2,1)S(1)}, u32[]{:S(2)}, u32[]{:S(2)}) %all-to-all-start) | async-done | bytes 1277984 | tf_op jit(solution)/shard_map/all_to_all | solution.py:317
  76.0 20.1 %all-gather.3.cloned.1.call-done = bf16[2048,2048]{1,0:T(8,128)(2,1)} async-done(((bf16[128,2048]{1,0:T(8,128)(2,1)}), bf16[2048,2048]{1,0:T(8,128)(2,1)}) %all-gather.3.cloned.1.call-update) | async-done | bytes 8388624 | tf_op jit(solution)/shard_map/all_gather | solution.py:313
  96.1 14.2 %experts.1 = (bf16[4,2,384,128]{3,2,1,0:T(8,128)(2,1)}, bf16[4,2,384,128]{3,2,1,0:T(8,128)(2,1)}, bf16[4,2,384,128]{3,2,1,0:T(8,128)(2,1)}, bf16[4,2,384,128]{3,...) custom-call(s32[3]{0:T(128)S(1)} %pad_add_fusion.at_ref, ...), custom_call_target="tpu_custom_call" | custom-call | flops 6400000000 | bytes 24000000 | tf_op jit(solution)/shard_map/experts/pallas_call | solution.py:255
  110.3 4.5 %all-to-all-start.1 = ((bf16[16,96,384]{2,1,0:T(8,128)(2,1)}), bf16[16,96,384]{2,1,0:T(8,128)(2,1)S(1)}, u32[]{:S(2)}, u32[]{:S(2)}) async-start(bf16[16,96,384]{2,1,0:T(8,128)(2,1)} %get-tuple-element.18), calls=%async_computation.1 | async-start | bytes 2359296 | tf_op jit(solution)/shard_map/all_to_all | solution.py:322
  114.9 0.6 collective-permute-start.12
  115.5 2.4 %collective-permute-start.13 = (bf16[4,2,384,128]{3,2,1,0:T(8,128)(2,1)}, bf16[4,2,384,128]{3,2,1,0:T(8,128)(2,1)S(1)}, u32[]{:S(2)}, u32[]{:S(2)}) collective-permute-start(bf16[4,2,384,128]{3,2,1,0:T(8,128)(2,1)} %get-tuple-element.23), channel_id=1, source_target_pairs={{0,128},{1,129},{2,130},{3,131},{4,132},{5,133},{6,134},{7,135},{8... | collective-permute-start | bytes 2359304 | tf_op jit(solution)/shard_map/ppermute | solution.py:199
  117.9 1.5 collective-permute-start.18
  119.4 2.7 %collective-permute-start.19 = (bf16[4,2,384,128]{3,2,1,0:T(8,128)(2,1)}, bf16[4,2,384,128]{3,2,1,0:T(8,128)(2,1)S(1)}, u32[]{:S(2)}, u32[]{:S(2)}) collective-permute-start(bf16[4,2,384,128]{3,2,1,0:T(8,128)(2,1)} %get-tuple-element.27), channel_id=1, source_target_pairs={{0,32},{1,33},{2,34},{3,35},{4,36},{5,37},{6,38},{7,39},{8,40},{9,... | collective-permute-start | bytes 2359304 | tf_op jit(solution)/shard_map/ppermute | solution.py:199
  122.1 13.4 %collective-permute-done.12 = bf16[4,2,384,128]{3,2,1,0:T(8,128)(2,1)S(1)} collective-permute-done((bf16[4,2,384,128]{3,2,1,0:T(8,128)(2,1)}, bf16[4,2,384,128]{3,2,1,0:T(8,128)(2,1)S(1)}, u32[]{:S(2)}, u32[]{:S(2)}) %collective-permute-start.12) | collective-permute-done | bytes 786464 | tf_op jit(solution)/shard_map/ppermute | solution.py:199
  135.5 2.7 %collective-permute-start.20 = (bf16[4,2,384,128]{3,2,1,0:T(8,128)(2,1)}, bf16[4,2,384,128]{3,2,1,0:T(8,128)(2,1)S(1)}, u32[]{:S(2)}, u32[]{:S(2)}) collective-permute-start(bf16[4,2,384,128]{3,2,1,0:T(8,128)(2,1)} %get-tuple-element.28), channel_id=1, source_target_pairs={{0,48},{1,49},{2,50},{3,51},{4,52},{5,53},{6,54},{7,55},{8,56},{9,... | collective-permute-start | bytes 2359304 | tf_op jit(solution)/shard_map/ppermute | solution.py:199
  138.3 15.3 %collective-permute-done.14 = bf16[4,2,384,128]{3,2,1,0:T(8,128)(2,1)S(1)} collective-permute-done((bf16[4,2,384,128]{3,2,1,0:T(8,128)(2,1)}, bf16[4,2,384,128]{3,2,1,0:T(8,128)(2,1)S(1)}, u32[]{:S(2)}, u32[]{:S(2)}) %collective-permute-start.14) | collective-permute-done | bytes 786464 | tf_op jit(solution)/shard_map/ppermute | solution.py:199
  153.6 1.2 fusion.3
  154.7 2.7 %collective-permute-start.17 = (bf16[2,384,128]{2,1,0:T(8,128)(2,1)S(1)}, bf16[2,384,128]{2,1,0:T(8,128)(2,1)S(1)}, u32[]{:S(2)}, u32[]{:S(2)}) collective-permute-start(bf16[2,384,128]{2,1,0:T(8,128)(2,1)S(1)} %get-tuple-element.33), channel_id=1, source_target_pairs={{0,48},{1,49},{2,50},{3,51},{4,52},{5,53},{6,54},{7,55},{8,56},{9,... | collective-permute-start | bytes 589832 | tf_op jit(solution)/shard_map/ppermute | solution.py:199
  157.5 0.8 collective-permute-start.16
  158.3 0.9 collective-permute-start.15
  159.2 1.2 fusion.7
  160.4 0.9 collective-permute-start.23
  161.3 1.5 collective-permute-start.22
  162.7 3.3 %collective-permute-done.17.refs_3_ = bf16[2,384,128]{2,1,0:T(8,128)(2,1)S(1)} collective-permute-done((bf16[2,384,128]{2,1,0:T(8,128)(2,1)S(1)}, bf16[2,384,128]{2,1,0:T(8,128)(2,1)S(1)}, u32[]{:S(2)}, u32[]{:S(2)}) %collective-permute-start.17) | collective-permute-done | bytes 196640 | tf_op jit(solution)/shard_map/ppermute | solution.py:199
  166.1 3.1 %unpack.1 = (bf16[1024,384]{1,0:T(8,128)(2,1)}, bf16[8,128]{1,0:T(8,128)(2,1)}) custom-call(s32[8,128]{1,0:T(8,128)S(1)} %bitcast.44, f32[8,128]{1,0:T(8,128)S(1)} %get-tuple-element.16.pos_ref, bf16[8,128]{1,0:T(8,128)(2,1)S(1)} %bitcast.46, bf16[1024,384]{1,0:T(8,128)(2,1)S(1)} %bitcast.42, bf16[1536,384]{1,0:T(8,128)(2,1)S(1)} %bitcast.39), custom_call_target="tpu_custom_call" | custom-call | flops 1207959552 | bytes 4194304 | tf_op jit(solution)/shard_map/unpack/pallas_call | solution.py:281
  169.2 0.7 collective-permute-done.15.refs_1_
  169.9 2.0 %collective-permute-done.23.refs_7_ = bf16[2,384,128]{2,1,0:T(8,128)(2,1)S(1)} collective-permute-done((bf16[2,384,128]{2,1,0:T(8,128)(2,1)}, bf16[2,384,128]{2,1,0:T(8,128)(2,1)S(1)}, u32[]{:S(2)}, u32[]{:S(2)}) %collective-permute-start.23) | collective-permute-done | bytes 196640 | tf_op jit(solution)/shard_map/ppermute | solution.py:199
  172.0 0.6 collective-permute-done.21.refs_5_
  172.6 0.7 copy-done
  173.3 1.2 finish.1
  (44 shorter events, 0.3 us)
Async XLA Ops:
  7.2 12.9 %copy-start.2 = (s32[128,8]{0,1:T(8,128)S(1)}, s32[128,8]{0,1:T(8,128)}, u32[]{:S(2)}) copy-start(s32[128,8]{0,1:T(8,128)} %param.8) | copy-start | bytes 12292
  7.2 12.9 %copy-start.3 = (bf16[128,8]{0,1:T(8,128)(2,1)S(1)}, bf16[128,8]{0,1:T(8,128)(2,1)}, u32[]{:S(2)}) copy-start(bf16[128,8]{0,1:T(8,128)(2,1)} %param.7) | copy-start | bytes 6148
  7.2 12.9 %copy-start.1 = (bf16[128,8,384]{2,1,0:T(8,128)(2,1)S(1)}, bf16[128,8,384]{2,1,0:T(8,128)(2,1)}, u32[]{:S(2)}) copy-start(bf16[128,8,384]{2,1,0:T(8,128)(2,1)} %param.6) | copy-start | bytes 2359300
  7.2 88.9 %all-gather.3.cloned.1.call-start = ((), (), s32[]{:S(2)}) async-start(), calls=%async_computation.2 | async-start | bytes 8912896 | tf_op jit(solution)/shard_map/all_gather | solution.py:313
  9.1 9.4 %collective-permute-start.1 = (bf16[2,128,384]{2,1,0:T(8,128)(2,1)S(1)}, bf16[2,128,384]{2,1,0:T(8,128)(2,1)S(1)}, u32[]{:S(2)}, u32[]{:S(2)}) collective-permute-start(bf16[2,128,384]{2,1,0:T(8,128)(2,1)S(1)} %get-tuple-element.40), channel_id=1, source_target_pairs={{0,128},{1,129},{2,130},{3,131},{4,132},{5,133},{6,134},{7,135},{8... | collective-permute-start | bytes 589832 | tf_op jit(solution)/shard_map/ppermute | solution.py:199
  10.5 21.3 %collective-permute-start = (bf16[2,128,384]{2,1,0:T(8,128)(2,1)S(1)}, bf16[2,128,384]{2,1,0:T(8,128)(2,1)S(1)}, u32[]{:S(2)}, u32[]{:S(2)}) collective-permute-start(bf16[2,128,384]{2,1,0:T(8,128)(2,1)S(1)} %get-tuple-element.40), channel_id=1, source_target_pairs={{0,192},{1,193},{2,194},{3,195},{4,196},{5,197},{6,198},{7,199},{8... | collective-permute-start | bytes 589832 | tf_op jit(solution)/shard_map/ppermute | solution.py:199
  12.2 19.6 %collective-permute-start.2 = (bf16[2,128,384]{2,1,0:T(8,128)(2,1)S(1)}, bf16[2,128,384]{2,1,0:T(8,128)(2,1)S(1)}, u32[]{:S(2)}, u32[]{:S(2)}) collective-permute-start(bf16[2,128,384]{2,1,0:T(8,128)(2,1)S(1)} %get-tuple-element.40), channel_id=1, source_target_pairs={{0,64},{1,65},{2,66},{3,67},{4,68},{5,69},{6,70},{7,71},{8,72},{9,... | collective-permute-start | bytes 589832 | tf_op jit(solution)/shard_map/ppermute | solution.py:199
  13.8 21.7 %collective-permute-start.7 = (bf16[2,128,384]{2,1,0:T(8,128)(2,1)S(1)}, bf16[2,128,384]{2,1,0:T(8,128)(2,1)}, u32[]{:S(2)}, u32[]{:S(2)}) collective-permute-start(bf16[2,128,384]{2,1,0:T(8,128)(2,1)S(1)} %get-tuple-element.39), channel_id=1, source_target_pairs={{0,32},{1,33},{2,34},{3,35},{4,36},{5,37},{6,38},{7,39},{8,40},{9,... | collective-permute-start | bytes 589832 | tf_op jit(solution)/shard_map/ppermute | solution.py:199
  17.0 18.5 %collective-permute-start.6 = (bf16[2,128,384]{2,1,0:T(8,128)(2,1)S(1)}, bf16[2,128,384]{2,1,0:T(8,128)(2,1)}, u32[]{:S(2)}, u32[]{:S(2)}) collective-permute-start(bf16[2,128,384]{2,1,0:T(8,128)(2,1)S(1)} %get-tuple-element.39), channel_id=1, source_target_pairs={{0,48},{1,49},{2,50},{3,51},{4,52},{5,53},{6,54},{7,55},{8,56},{9,... | collective-permute-start | bytes 589832 | tf_op jit(solution)/shard_map/ppermute | solution.py:199
  18.5 4.8 %copy-start.8 = (bf16[2,128,384]{2,1,0:T(8,128)(2,1)}, bf16[2,128,384]{2,1,0:T(8,128)(2,1)S(1)}, u32[]{:S(2)}) copy-start(bf16[2,128,384]{2,1,0:T(8,128)(2,1)S(1)} %collective-permute-done.1) | copy-start | bytes 589828
  18.5 17.0 %collective-permute-start.8 = (bf16[2,128,384]{2,1,0:T(8,128)(2,1)S(1)}, bf16[2,128,384]{2,1,0:T(8,128)(2,1)}, u32[]{:S(2)}, u32[]{:S(2)}) collective-permute-start(bf16[2,128,384]{2,1,0:T(8,128)(2,1)S(1)} %get-tuple-element.39), channel_id=1, source_target_pairs={{0,16},{1,17},{2,18},{3,19},{4,20},{5,21},{6,22},{7,23},{8,24},{9,... | collective-permute-start | bytes 589832 | tf_op jit(solution)/shard_map/ppermute | solution.py:199
  23.2 52.8 %all-to-all-start = ((bf16[16,104,384]{2,1,0:T(8,128)(2,1)}), bf16[16,104,384]{2,1,0:T(8,128)(2,1)S(1)}, u32[]{:S(2)}, u32[]{:S(2)}) async-start(bf16[16,104,384]{2,1,0:T(8,128)(2,1)} %get-tuple-element.17), calls=%async_computation | async-start | bytes 2555904 | tf_op jit(solution)/shard_map/all_to_all | solution.py:317
  31.8 0.7 copy-start.9
  31.8 0.7 copy-start.10
  33.9 62.2 %copy-start.4 = (bf16[4,2,128,384]{3,2,1,0:T(8,128)(2,1)}, bf16[4,2,128,384]{3,2,1,0:T(8,128)(2,1)S(1)}, u32[]{:S(2)}) copy-start(bf16[4,2,128,384]{3,2,1,0:T(8,128)(2,1)S(1)} %pad_maximum_fusion.refs_0_) | copy-start | bytes 2359300
  33.9 13.3 %collective-permute-start.3 = (bf16[4,2,128,384]{3,2,1,0:T(8,128)(2,1)S(1)}, bf16[4,2,128,384]{3,2,1,0:T(8,128)(2,1)S(1)}, u32[]{:S(2)}, u32[]{:S(2)}) collective-permute-start(bf16[4,2,128,384]{3,2,1,0:T(8,128)(2,1)S(1)} %pad_maximum_fusion.refs_0_), channel_id=1, source_target_pairs={{0,16},{1,49},{2,18},{3,51},{4,20},{5,53},{6,22},{7,55},{8,24},{9,... | collective-permute-start | bytes 2359304 | tf_op jit(solution)/shard_map/ppermute | solution.py:199
  36.8 10.4 %copy-start.5 = (bf16[4,2,128,384]{3,2,1,0:T(8,128)(2,1)}, bf16[4,2,128,384]{3,2,1,0:T(8,128)(2,1)S(1)}, u32[]{:S(2)}) copy-start(bf16[4,2,128,384]{3,2,1,0:T(8,128)(2,1)S(1)} %pad_maximum_fusion.1.refs_4_) | copy-start | bytes 2359300
  36.8 12.1 %collective-permute-start.9 = (bf16[4,2,128,384]{3,2,1,0:T(8,128)(2,1)S(1)}, bf16[4,2,128,384]{3,2,1,0:T(8,128)(2,1)S(1)}, u32[]{:S(2)}, u32[]{:S(2)}) collective-permute-start(bf16[4,2,128,384]{3,2,1,0:T(8,128)(2,1)S(1)} %pad_maximum_fusion.1.refs_4_), channel_id=1, source_target_pairs={{0,64},{1,193},{2,66},{3,195},{4,68},{5,197},{6,70},{7,199},{8,72}... | collective-permute-start | bytes 2359304 | tf_op jit(solution)/shard_map/ppermute | solution.py:199
  47.2 1.7 copy-start.11
  47.2 13.3 %collective-permute-start.4 = (bf16[4,2,128,384]{3,2,1,0:T(8,128)(2,1)S(1)}, bf16[4,2,128,384]{3,2,1,0:T(8,128)(2,1)}, u32[]{:S(2)}, u32[]{:S(2)}) collective-permute-start(bf16[4,2,128,384]{3,2,1,0:T(8,128)(2,1)S(1)} %collective-permute-done.3.refs_1_), channel_id=1, source_target_pairs={{0,16},{1,49},{2,18},{3,51},{4,20},{5,53},{6,22},{7,55},{8,24},{9,... | collective-permute-start | bytes 2359304 | tf_op jit(solution)/shard_map/ppermute | solution.py:199
  48.8 11.6 %copy-start.12 = (bf16[4,2,128,384]{3,2,1,0:T(8,128)(2,1)}, bf16[4,2,128,384]{3,2,1,0:T(8,128)(2,1)S(1)}, u32[]{:S(2)}) copy-start(bf16[4,2,128,384]{3,2,1,0:T(8,128)(2,1)S(1)} %collective-permute-done.9.refs_5_) | copy-start | bytes 2359300
  48.8 12.1 %collective-permute-start.10 = (bf16[4,2,128,384]{3,2,1,0:T(8,128)(2,1)S(1)}, bf16[4,2,128,384]{3,2,1,0:T(8,128)(2,1)}, u32[]{:S(2)}, u32[]{:S(2)}) collective-permute-start(bf16[4,2,128,384]{3,2,1,0:T(8,128)(2,1)S(1)} %collective-permute-done.9.refs_5_), channel_id=1, source_target_pairs={{0,64},{1,193},{2,66},{3,195},{4,68},{5,197},{6,70},{7,199},{8,72}... | collective-permute-start | bytes 2359304 | tf_op jit(solution)/shard_map/ppermute | solution.py:199
  60.5 15.6 %collective-permute-start.5 = (bf16[4,2,128,384]{3,2,1,0:T(8,128)(2,1)}, bf16[4,2,128,384]{3,2,1,0:T(8,128)(2,1)}, u32[]{:S(2)}, u32[]{:S(2)}) collective-permute-start(bf16[4,2,128,384]{3,2,1,0:T(8,128)(2,1)} %collective-permute-done.4.refs_2_), channel_id=1, source_target_pairs={{0,16},{1,49},{2,18},{3,51},{4,20},{5,53},{6,22},{7,55},{8,24},{9,... | collective-permute-start | bytes 2359304 | tf_op jit(solution)/shard_map/ppermute | solution.py:199
  60.9 15.1 %collective-permute-start.11 = (bf16[4,2,128,384]{3,2,1,0:T(8,128)(2,1)}, bf16[4,2,128,384]{3,2,1,0:T(8,128)(2,1)}, u32[]{:S(2)}, u32[]{:S(2)}) collective-permute-start(bf16[4,2,128,384]{3,2,1,0:T(8,128)(2,1)} %collective-permute-done.10.refs_6_), channel_id=1, source_target_pairs={{0,64},{1,193},{2,66},{3,195},{4,68},{5,197},{6,70},{7,199},{8,72}... | collective-permute-start | bytes 2359304 | tf_op jit(solution)/shard_map/ppermute | solution.py:199
  110.3 43.2 %copy-start.7 = (bf16[4,2,384,128]{3,2,1,0:T(8,128)(2,1)S(1)}, bf16[4,2,384,128]{3,2,1,0:T(8,128)(2,1)}, u32[]{:S(2)}) copy-start(bf16[4,2,384,128]{3,2,1,0:T(8,128)(2,1)} %get-tuple-element.21) | copy-start | bytes 2359300
  110.3 55.7 %all-to-all-start.1 = ((bf16[16,96,384]{2,1,0:T(8,128)(2,1)}), bf16[16,96,384]{2,1,0:T(8,128)(2,1)S(1)}, u32[]{:S(2)}, u32[]{:S(2)}) async-start(bf16[16,96,384]{2,1,0:T(8,128)(2,1)} %get-tuple-element.18), calls=%async_computation.1 | async-start | bytes 2359296 | tf_op jit(solution)/shard_map/all_to_all | solution.py:322
  114.9 20.6 %collective-permute-start.12 = (bf16[4,2,384,128]{3,2,1,0:T(8,128)(2,1)}, bf16[4,2,384,128]{3,2,1,0:T(8,128)(2,1)S(1)}, u32[]{:S(2)}, u32[]{:S(2)}) collective-permute-start(bf16[4,2,384,128]{3,2,1,0:T(8,128)(2,1)} %get-tuple-element.22), channel_id=1, source_target_pairs={{0,64},{1,65},{2,66},{3,67},{4,68},{5,69},{6,70},{7,71},{8,72},{9,... | collective-permute-start | bytes 2359304 | tf_op jit(solution)/shard_map/ppermute | solution.py:199
  115.5 22.8 %collective-permute-start.13 = (bf16[4,2,384,128]{3,2,1,0:T(8,128)(2,1)}, bf16[4,2,384,128]{3,2,1,0:T(8,128)(2,1)S(1)}, u32[]{:S(2)}, u32[]{:S(2)}) collective-permute-start(bf16[4,2,384,128]{3,2,1,0:T(8,128)(2,1)} %get-tuple-element.23), channel_id=1, source_target_pairs={{0,128},{1,129},{2,130},{3,131},{4,132},{5,133},{6,134},{7,135},{8... | collective-permute-start | bytes 2359304 | tf_op jit(solution)/shard_map/ppermute | solution.py:199
  117.9 35.7 %collective-permute-start.14 = (bf16[4,2,384,128]{3,2,1,0:T(8,128)(2,1)}, bf16[4,2,384,128]{3,2,1,0:T(8,128)(2,1)S(1)}, u32[]{:S(2)}, u32[]{:S(2)}) collective-permute-start(bf16[4,2,384,128]{3,2,1,0:T(8,128)(2,1)} %get-tuple-element.24), channel_id=1, source_target_pairs={{0,192},{1,193},{2,194},{3,195},{4,196},{5,197},{6,198},{7,199},{8... | collective-permute-start | bytes 2359304 | tf_op jit(solution)/shard_map/ppermute | solution.py:199
  117.9 40.4 %collective-permute-start.18 = (bf16[4,2,384,128]{3,2,1,0:T(8,128)(2,1)}, bf16[4,2,384,128]{3,2,1,0:T(8,128)(2,1)S(1)}, u32[]{:S(2)}, u32[]{:S(2)}) collective-permute-start(bf16[4,2,384,128]{3,2,1,0:T(8,128)(2,1)} %get-tuple-element.26), channel_id=1, source_target_pairs={{0,16},{1,17},{2,18},{3,19},{4,20},{5,21},{6,22},{7,23},{8,24},{9,... | collective-permute-start | bytes 2359304 | tf_op jit(solution)/shard_map/ppermute | solution.py:199
  119.4 39.8 %collective-permute-start.19 = (bf16[4,2,384,128]{3,2,1,0:T(8,128)(2,1)}, bf16[4,2,384,128]{3,2,1,0:T(8,128)(2,1)S(1)}, u32[]{:S(2)}, u32[]{:S(2)}) collective-permute-start(bf16[4,2,384,128]{3,2,1,0:T(8,128)(2,1)} %get-tuple-element.27), channel_id=1, source_target_pairs={{0,32},{1,33},{2,34},{3,35},{4,36},{5,37},{6,38},{7,39},{8,40},{9,... | collective-permute-start | bytes 2359304 | tf_op jit(solution)/shard_map/ppermute | solution.py:199
  135.5 23.6 %collective-permute-start.20 = (bf16[4,2,384,128]{3,2,1,0:T(8,128)(2,1)}, bf16[4,2,384,128]{3,2,1,0:T(8,128)(2,1)S(1)}, u32[]{:S(2)}, u32[]{:S(2)}) collective-permute-start(bf16[4,2,384,128]{3,2,1,0:T(8,128)(2,1)} %get-tuple-element.28), channel_id=1, source_target_pairs={{0,48},{1,49},{2,50},{3,51},{4,52},{5,53},{6,54},{7,55},{8,56},{9,... | collective-permute-start | bytes 2359304 | tf_op jit(solution)/shard_map/ppermute | solution.py:199
  153.6 5.6 %copy-start.6 = (bf16[4,2,384,128]{3,2,1,0:T(8,128)(2,1)S(1)}, bf16[4,2,384,128]{3,2,1,0:T(8,128)(2,1)}, u32[]{:S(2)}) copy-start(bf16[4,2,384,128]{3,2,1,0:T(8,128)(2,1)} %get-tuple-element.25) | copy-start | bytes 2359300
  154.7 11.3 %collective-permute-start.17 = (bf16[2,384,128]{2,1,0:T(8,128)(2,1)S(1)}, bf16[2,384,128]{2,1,0:T(8,128)(2,1)S(1)}, u32[]{:S(2)}, u32[]{:S(2)}) collective-permute-start(bf16[2,384,128]{2,1,0:T(8,128)(2,1)S(1)} %get-tuple-element.33), channel_id=1, source_target_pairs={{0,48},{1,49},{2,50},{3,51},{4,52},{5,53},{6,54},{7,55},{8,56},{9,... | collective-permute-start | bytes 589832 | tf_op jit(solution)/shard_map/ppermute | solution.py:199
  157.5 11.7 %collective-permute-start.16 = (bf16[2,384,128]{2,1,0:T(8,128)(2,1)}, bf16[2,384,128]{2,1,0:T(8,128)(2,1)S(1)}, u32[]{:S(2)}, u32[]{:S(2)}) collective-permute-start(bf16[2,384,128]{2,1,0:T(8,128)(2,1)} %get-tuple-element.34), channel_id=1, source_target_pairs={{0,32},{1,33},{2,34},{3,35},{4,36},{5,37},{6,38},{7,39},{8,40},{9,... | collective-permute-start | bytes 589832 | tf_op jit(solution)/shard_map/ppermute | solution.py:199
  158.3 11.7 %collective-permute-start.15 = (bf16[2,384,128]{2,1,0:T(8,128)(2,1)}, bf16[2,384,128]{2,1,0:T(8,128)(2,1)S(1)}, u32[]{:S(2)}, u32[]{:S(2)}) collective-permute-start(bf16[2,384,128]{2,1,0:T(8,128)(2,1)} %get-tuple-element.35), channel_id=1, source_target_pairs={{0,16},{1,17},{2,18},{3,19},{4,20},{5,21},{6,22},{7,23},{8,24},{9,... | collective-permute-start | bytes 589832 | tf_op jit(solution)/shard_map/ppermute | solution.py:199
  160.4 11.6 %collective-permute-start.23 = (bf16[2,384,128]{2,1,0:T(8,128)(2,1)}, bf16[2,384,128]{2,1,0:T(8,128)(2,1)S(1)}, u32[]{:S(2)}, u32[]{:S(2)}) collective-permute-start(bf16[2,384,128]{2,1,0:T(8,128)(2,1)} %get-tuple-element.29), channel_id=1, source_target_pairs={{0,192},{1,193},{2,194},{3,195},{4,196},{5,197},{6,198},{7,199},{8... | collective-permute-start | bytes 589832 | tf_op jit(solution)/shard_map/ppermute | solution.py:199
  161.3 10.7 %collective-permute-start.22 = (bf16[2,384,128]{2,1,0:T(8,128)(2,1)}, bf16[2,384,128]{2,1,0:T(8,128)(2,1)S(1)}, u32[]{:S(2)}, u32[]{:S(2)}) collective-permute-start(bf16[2,384,128]{2,1,0:T(8,128)(2,1)} %get-tuple-element.30), channel_id=1, source_target_pairs={{0,128},{1,129},{2,130},{3,131},{4,132},{5,133},{6,134},{7,135},{8... | collective-permute-start | bytes 589832 | tf_op jit(solution)/shard_map/ppermute | solution.py:199
  166.1 6.5 %collective-permute-start.21 = (bf16[2,384,128]{2,1,0:T(8,128)(2,1)}, bf16[2,384,128]{2,1,0:T(8,128)(2,1)S(1)}, u32[]{:S(2)}, u32[]{:S(2)}) collective-permute-start(bf16[2,384,128]{2,1,0:T(8,128)(2,1)} %get-tuple-element.31), channel_id=1, source_target_pairs={{0,64},{1,65},{2,66},{3,67},{4,68},{5,69},{6,70},{7,71},{8,72},{9,... | collective-permute-start | bytes 589832 | tf_op jit(solution)/shard_map/ppermute | solution.py:199
  172.6 0.7 copy-start
Sparse Core Ops, SparseCore 0:
  9.9 86.1 all-gather.2

commit v2 on v1

--- a/solution.py
+++ b/solution.py
@@ -10,6 +10,8 @@
 CAP = 24
 SIDE = 4
 EXTRA = 8
+HIDDEN_FLOPS = 2.4e9
+SUM_FLOPS = 6e9
 BF16, F32, I32 = jnp.bfloat16, jnp.float32, jnp.int32
 
 
@@ -19,6 +21,10 @@
 
 def dot(a, b):
     return jnp.dot(a, b, preferred_element_type=F32)
+
+
+def add(*parts):
+    return sum(p.astype(F32) for p in parts)
 
 
 def pack_kernel(owners, local, ids_ref, gate_ref, hidden_ref, wire_ref, pos_ref):
@@ -62,11 +68,14 @@
             ).astype(BF16)
 
 
+ROLE = {(0, 2): 0, (1, 1): 1, (1, 2): 2, (0, 3): 3, (0, 1): 4, (1, 3): 5, (0, 0): 6, (1, 0): 7}
+
+
 def expert_kernel(local, at_ref, wire_ref, grad_hbm, *refs):
     half = local // 2
-    pieces, refs = refs[: 2 * SIDE], refs[2 * SIDE :]
-    messages, u_hbm = refs[: 2 * SIDE], refs[2 * SIDE]
-    gbuf, xbuf, abuf, wbuf, ubuf, obuf, gsem, wsem, msem, usem = refs[2 * SIDE + 1 :]
+    refs = refs[2:]
+    messages, x_hbm = refs[: 2 * SIDE], refs[2 * SIDE]
+    gbuf, xbuf, abuf, gsem, msem, xsem = refs[2 * SIDE + 1 :]
     owners, tokens, model = gbuf.shape
     width = wire_ref.shape[2]
     depth = model // (SIDE * SIDE)
@@ -75,18 +84,7 @@
         pltpu.make_async_copy(grad_hbm.at[pl.ds(2 * p, 2)], gbuf.at[pl.ds(2 * p, 2)], gsem.at[p])
         for p in range(chips)
     ]
-    weights = [
-        [
-            pltpu.make_async_copy(
-                pieces[h * SIDE + k],
-                wbuf.at[h, at_ref[2] * k + (1 - at_ref[2]) * ((SIDE - k) % SIDE)],
-                wsem.at[h, k],
-            )
-            for k in range(SIDE)
-        ]
-        for h in range(2)
-    ]
-    for c in loads + weights[0] + weights[1]:
+    for c in loads:
         c.start()
     places = []
     for d in range(SIDE * SIDE):
@@ -115,7 +113,8 @@
                 xbuf[e, p * block : (p + 1) * block, pl.ds(places[d], depth)] = rows[
                     e * block : (e + 1) * block, d * depth : (d + 1) * depth
                 ]
-    copies = []
+    copies = [pltpu.make_async_copy(xbuf, x_hbm, xsem)]
+    copies[0].start()
     wire = wire_ref[:, : local * CAP, :].astype(F32)
     step = SIDE * depth
     for e in range(local):
@@ -126,15 +125,40 @@
             grad = dot(hidden, xbuf[e, :, dx * step : (dx + 1) * step]).astype(BF16)
             for dy in range(SIDE):
                 a, b = (dx, dy) if h == 0 else (dy, dx)
-                abuf[h, a, b, e % half] = grad[:, dy * depth : (dy + 1) * depth]
+                abuf[h, ROLE[e % half, a], b] = grad[:, dy * depth : (dy + 1) * depth]
         if e % half == half - 1:
-            for a in range(SIDE):
-                copies.append(
-                    pltpu.make_async_copy(abuf.at[h, a], messages[h * SIDE + a], msem.at[h, a])
-                )
+            for m in range(SIDE):
+                block_pair = abuf.at[h, pl.ds(2 * m, 2)]
+                copies.append(pltpu.make_async_copy(block_pair, messages[h * SIDE + m], msem.at[h, m]))
                 copies[-1].start()
+    for c in copies:
+        c.wait()
+
+
+def hidden_kernel(local, at_ref, x_hbm, *refs):
+    half = local // 2
+    pieces, refs = refs[: 2 * SIDE], refs[2 * SIDE :]
+    u_hbm, xbuf, wbuf, ubuf, obuf, xsem, wsem, usem = refs
+    owners, _, width = ubuf.shape
+    step = xbuf.shape[2] // SIDE
+    rows = [pltpu.make_async_copy(x_hbm.at[e], xbuf.at[e], xsem.at[e]) for e in range(local)]
+    weights = [
+        [
+            pltpu.make_async_copy(
+                pieces[h * SIDE + k],
+                wbuf.at[h, at_ref[2] * k + (1 - at_ref[2]) * ((SIDE - k) % SIDE)],
+                wsem.at[h, k],
+            )
+            for k in range(SIDE)
+        ]
+        for h in range(2)
+    ]
+    for h in range(2):
+        for c in weights[h] + rows[h * half : (h + 1) * half]:
+            c.start()
     for e in range(local):
         h = e // half
+        rows[e].wait()
         if e % half == 0:
             for c in weights[h]:
                 c.wait()
@@ -144,10 +168,9 @@
             u += dot(xbuf[e, :, dx * step : (dx + 1) * step], w.reshape(step, width))
         ubuf[:, e * CAP : (e + 1) * CAP, :] = u.reshape(owners, CAP, width)
     obuf[...] = ubuf[...].astype(BF16)
-    copies.append(pltpu.make_async_copy(obuf, u_hbm, usem))
-    copies[-1].start()
-    for c in copies:
-        c.wait()
+    out = pltpu.make_async_copy(obuf, u_hbm, usem)
+    out.start()
+    out.wait()
 
 
 def unpack_kernel(ids_ref, pos_ref, gate_ref, hidden_ref, back_ref, out_ref, gate_out_ref):
@@ -178,6 +201,15 @@
     ).astype(BF16)
 
 
+def sum_kernel(*refs):
+    for h in range(2):
+        own, on, back, on_later, back_later = refs[5 * h : 5 * h + 5]
+        outs = refs[10 + SIDE * h : 10 + SIDE * (h + 1)]
+        for d in range(SIDE):
+            outs[d][0] = add(own[0, d], back[1, d], on_later[d]).astype(BF16)
+            outs[d][1] = add(own[1, d], on[1, d], back_later[d]).astype(BF16)
+
+
 def finish_kernel(after_ref, *refs):
     out_ref = refs[-1]
     half = out_ref.shape[1] // 2
@@ -206,14 +238,20 @@
     return [pltpu.with_memory_space_constraint(b, pltpu.HBM) for b in blocks]
 
 
-def add(*parts):
-    return sum(p.astype(F32) for p in parts)
-
-
-def scatter_half(messages, first):
-    got = [messages[0]] + [shift(messages[d], first, d) for d in range(1, SIDE)]
-    sums = [add(*[g[d] for g in got]).astype(BF16) for d in range(SIDE)]
-    return [sums[0]] + [shift(sums[d], 1 - first, d) for d in range(1, SIDE)]
+def scatter(messages):
+    got = []
+    for h in range(2):
+        on, back, later, own = messages[h]
+        on, back = shift(on, h, 1), shift(back, h, -1)
+        on_later = shift(add(later[0], on[0]).astype(BF16), h, 1)
+        back_later = shift(add(later[1], back[0]).astype(BF16), h, -1)
+        got += [own, on, back, on_later, back_later]
+    sums = sum_call(got)
+    out = []
+    for h in range(2):
+        mine = sums[h * SIDE : (h + 1) * SIDE]
+        out += [mine[0]] + [shift(mine[d], 1 - h, d) for d in range(1, SIDE)]
+    return out
 
 
 VMEM = pl.BlockSpec(memory_space=pltpu.VMEM)
@@ -247,33 +285,66 @@
     )(ids, gate, hidden)
 
 
-def expert_call(local, at, wire, grads, pieces):
+def expert_call(local, at, wire, grads, after):
     owners, tokens, model = grads.shape
     width = wire.shape[2]
     depth = model // (SIDE * SIDE)
     rows = owners * CAP
     return pl.pallas_call(
         functools.partial(expert_kernel, local),
-        out_shape=[pltpu.HBM((SIDE, local // 2, width, depth), BF16)] * (2 * SIDE)
-        + [pltpu.HBM((owners, local * CAP, width), BF16)],
-        in_specs=[SMEM, VMEM] + [HBM] * (1 + len(pieces)),
+        out_shape=[pltpu.HBM((2, SIDE, width, depth), BF16)] * (2 * SIDE)
+        + [pltpu.HBM((local, rows, model), BF16)],
+        in_specs=[SMEM, VMEM, HBM] + [HBM] * len(after),
         out_specs=[HBM] * (2 * SIDE + 1),
         scratch_shapes=[
             pltpu.VMEM((owners, tokens, model), BF16),
             pltpu.VMEM((local, rows, model), BF16),
-            pltpu.VMEM((2, SIDE, SIDE, local // 2, width, depth), BF16),
+            pltpu.VMEM((2, 2 * SIDE, SIDE, width, depth), BF16),
+            pltpu.SemaphoreType.DMA((owners // 2,)),
+            pltpu.SemaphoreType.DMA((2, SIDE)),
+            pltpu.SemaphoreType.DMA,
+        ],
+        compiler_params=params(36),
+        cost_estimate=cost(4e9, 22e6),
+        name="experts",
+    )(at, wire, pltpu.with_memory_space_constraint(grads, pltpu.HBM), *after)
+
+
+def hidden_call(local, at, x, pieces):
+    _, rows, model = x.shape
+    depth, width = pieces[0].shape[2:]
+    owners = rows // CAP
+    return pl.pallas_call(
+        functools.partial(hidden_kernel, local),
+        out_shape=pltpu.HBM((owners, local * CAP, width), BF16),
+        in_specs=[SMEM] + [HBM] * (1 + len(pieces)),
+        out_specs=HBM,
+        scratch_shapes=[
+            pltpu.VMEM((local, rows, model), BF16),
             pltpu.VMEM((2, SIDE, SIDE, local // 2, depth, width), BF16),
             pltpu.VMEM((owners, local * CAP, width), F32),
             pltpu.VMEM((owners, local * CAP, width), BF16),
-            pltpu.SemaphoreType.DMA((owners // 2,)),
-            pltpu.SemaphoreType.DMA((2, SIDE)),
+            pltpu.SemaphoreType.DMA((local,)),
             pltpu.SemaphoreType.DMA((2, SIDE)),
             pltpu.SemaphoreType.DMA,
         ],
-        compiler_params=params(40),
-        cost_estimate=cost(6.4e9, 24e6),
-        name="experts",
-    )(at, wire, pltpu.with_memory_space_constraint(grads, pltpu.HBM), *pieces)
+        compiler_params=params(28),
+        cost_estimate=cost(HIDDEN_FLOPS, 14e6),
+        name="hidden_grad",
+    )(at, x, *pieces)
+
+
+def sum_call(parts):
+    _, _, width, depth = parts[0].shape
+    return pl.pallas_call(
+        sum_kernel,
+        out_shape=[sds((2, width, depth), BF16)] * (2 * SIDE),
+        in_specs=[VMEM] * len(parts),
+        out_specs=[VMEM] * (2 * SIDE),
+        compiler_params=params(24),
+        cost_estimate=cost(SUM_FLOPS, 4e6),
+        name="sum_parts",
+    )(*parts)
 
 
 def unpack(ids, pos, gate, hidden, back):
@@ -318,9 +389,10 @@
     weights = down_weight.transpose(1, 0, 2)
     pieces = gather_half(weights[:half], 0) + gather_half(weights[half:], 1)
 
-    *messages, u = expert_call(local, at, wire, grads, pieces)
+    *messages, x = expert_call(local, at, wire, grads, (pieces[SIDE - 1], pieces[-1]))
+    u = hidden_call(local, at, x, pieces)
     back = lax.all_to_all(u, "expert", split_axis=0, concat_axis=0, tiled=True)
-    sums = scatter_half(messages[:SIDE], 0) + scatter_half(messages[SIDE:], 1)
+    sums = scatter((messages[:SIDE], messages[SIDE:]))
     back = back.reshape(owners * local * CAP, width)
     grad_hidden, grad_gate = unpack(ids, pos, gate, hidden, back)
     grad_down = finish(sums, grad_gate, depth, local, width)

time: 184 us -> 179 us (0.973); the launches traced: 181 us -> 178 us
  waiting for transfers between devices: 90.3 us -> 77.9 us
  Pallas kernels: 21.8 us -> 29.3 us
  local copies, waits for them, and re-layouts: 2.55 us -> 8.36 us
  other arithmetic: 4.96 us -> 2.96 us
  starting transfers between devices: 47.5 us -> 45.5 us
    ppermute x24 -> x26, waiting for transfers between devices: 57.5 us -> 42.6 us  [shift(): return lax.ppermute(x, ('dp', 'expert'), pairs)]
    pallas_call x0 -> x2, Pallas kernels: none -> 9.95 us  [the longest x1 7.51 us: hidden_call(): pl.pallas_call(functools.partial(hidden_kernel, local), out_shape=pltpu.H...]
    unnamed x27 -> x39, local copies, waits for them, and re-layouts: 2.48 us -> 8.28 us
    convert_element_type x0 -> x2, other arithmetic: none -> 2.63 us  [scatter(): back_later = shift(add(later[1], back[0]).astype(BF16), h, -1)]
    all_to_all x1, waiting for transfers between devices: 12.1 us -> 14.4 us  [per_device(): lax.all_to_all(wire, 'expert', split_axis=0, concat_axis=0, tiled=True)]
    pallas_call x1, Pallas kernels: 14.2 us -> 11.9 us  [expert_call(): pl.pallas_call(functools.partial(expert_kernel, local), out_shape=[pltpu....]
    add x2 -> x0, other arithmetic: 2.33 us -> none  [add(): return sum((p.astype(F32) for p in parts))]
    another operation x2, other arithmetic: 2.55 us -> 0.25 us  [gather_half(): jnp.stack([weights] + [shift(weights, first, -d) for d in range(1, SIDE)])]
  transfers between devices with their start and end apart: 27 -> 29, of which waited for: 13 -> 12; matrix products, arithmetic and copies ran while one was open for 3% -> 2% of each run, Pallas kernels for 3% -> 9%
where the time goes in v2:
time: 179 us; the launch traced here: 178 us
  waiting for transfers between devices  77.9 us (44%)
  starting transfers between devices  45.5 us (25%)
  Pallas kernels  29.3 us (16%)
  between operations  14.3 us (8%)
  local copies, waits for them, and re-layouts  8.36 us (5%)
  other arithmetic  2.96 us (2%)
    ppermute x26, waiting for transfers between devices, shift(): return lax.ppermute(x, ('dp', 'expert'), pairs)  42.6 us
    ppermute x26, starting transfers between devices, shift(): return lax.ppermute(x, ('dp', 'expert'), pairs)  32.5 us
    all_gather x1, waiting for transfers between devices, per_device(): grads = lax.all_gather(out_grad, 'expert', axis=0, tiled=False)  20.1 us
    all_to_all x1, waiting for transfers between devices, per_device(): lax.all_to_all(wire, 'expert', split_axis=0, concat_axis=0, tiled=True)  14.4 us
    pallas_call x1, Pallas kernels, expert_call(): pl.pallas_call(functools.partial(expert_kernel, local), out_shape=[pltpu....  11.9 us
    all_to_all x1, starting transfers between devices, per_device(): lax.all_to_all(wire, 'expert', split_axis=0, concat_axis=0, tiled=True)  8.57 us
    unnamed x39, local copies, waits for them, and re-layouts  8.28 us
    pallas_call x1, Pallas kernels, hidden_call(): pl.pallas_call(functools.partial(hidden_kernel, local), out_shape=pltpu.H...  7.51 us
  transfers between devices with their start and end apart: 29, of which 12 were waited for; matrix products, arithmetic and copies ran while one was open for 2% of the time, Pallas kernels for 9%

profile of v2, /device:TPU:6, one launch (start us, length us, event | category | flops | bytes accessed | tf_op | source)
XLA Modules:
  0.0 178.3 jit_solution(15054070930477337626)
XLA Ops:
  7.2 0.7 all-gather.3.cloned.1.call-update
  7.9 1.0 copy.10
  9.1 1.5 collective-permute-start.1
  10.6 1.7 collective-permute-start
  12.2 1.6 collective-permute-start.2
  13.8 3.2 %collective-permute-start.7 = (bf16[2,128,384]{2,1,0:T(8,128)(2,1)S(1)}, bf16[2,128,384]{2,1,0:T(8,128)(2,1)S(1)}, u32[]{:S(2)}, u32[]{:S(2)}) collective-permute-start(bf16[2,128,384]{2,1,0:T(8,128)(2,1)S(1)} %get-tuple-element.51), channel_id=1, source_target_pairs={{0,32},{1,33},{2,34},{3,35},{4,36},{5,37},{6,38},{7,39},{8,40},{9,... | collective-permute-start | bytes 589832 | tf_op jit(solution)/shard_map/ppermute | solution.py:231
  17.0 1.1 collective-permute-start.6
  18.0 0.4 collective-permute-done.1
  18.5 1.6 collective-permute-start.8
  20.1 3.1 %pack.1 = (bf16[16,104,384]{2,1,0:T(8,128)(2,1)}, f32[8,128]{1,0:T(8,128)S(1)}) custom-call(s32[8,128]{1,0:T(8,128)S(1)} %bitcast.35, bf16[8,128]{1,0:T(8,128)(2,1)S(1)} %bitcast.37, bf16[1024,384]{1,0:T(8,128)(2,1)S(1)} %bitcast.33), custom_call_target="tpu_custom_call" | custom-call | flops 1207959552 | bytes 4194304 | tf_op jit(solution)/shard_map/pack/pallas_call | solution.py:277
  23.2 8.6 %all-to-all-start = ((bf16[16,104,384]{2,1,0:T(8,128)(2,1)}), bf16[16,104,384]{2,1,0:T(8,128)(2,1)S(1)}, u32[]{:S(2)}, u32[]{:S(2)}) async-start(bf16[16,104,384]{2,1,0:T(8,128)(2,1)} %get-tuple-element.25), calls=%async_computation | async-start | bytes 2555904 | tf_op jit(solution)/shard_map/all_to_all | solution.py:388
  31.9 0.9 copy-done.12
  32.8 1.6 collective-permute-start.3
  34.6 0.5 collective-permute-start.9
  35.1 11.0 %collective-permute-done.3.refs_1_ = bf16[4,2,128,384]{3,2,1,0:T(8,128)(2,1)S(1)} collective-permute-done((bf16[4,2,128,384]{3,2,1,0:T(8,128)(2,1)S(1)}, bf16[4,2,128,384]{3,2,1,0:T(8,128)(2,1)S(1)}, u32[]{:S(2)}, u32[]{:S(2)}) %collective-permute-start.3) | collective-permute-done | bytes 786464 | tf_op jit(solution)/shard_map/ppermute | solution.py:231
  47.0 1.3 collective-permute-start.10
  48.3 11.0 %collective-permute-done.4.refs_2_ = bf16[4,2,128,384]{3,2,1,0:T(8,128)(2,1)S(1)} collective-permute-done((bf16[4,2,128,384]{3,2,1,0:T(8,128)(2,1)S(1)}, bf16[4,2,128,384]{3,2,1,0:T(8,128)(2,1)S(1)}, u32[]{:S(2)}, u32[]{:S(2)}) %collective-permute-start.4) | collective-permute-done | bytes 786464 | tf_op jit(solution)/shard_map/ppermute | solution.py:231
  59.3 2.2 %collective-permute-start.11 = (bf16[4,2,128,384]{3,2,1,0:T(8,128)(2,1)S(1)}, bf16[4,2,128,384]{3,2,1,0:T(8,128)(2,1)}, u32[]{:S(2)}, u32[]{:S(2)}) collective-permute-start(bf16[4,2,128,384]{3,2,1,0:T(8,128)(2,1)S(1)} %collective-permute-done.10.refs_6_), channel_id=1, source_target_pairs={{0,64},{1,193},{2,66},{3,195},{4,68},{5,197},{6,70},{7,199},{8,72}... | collective-permute-start | bytes 2359304 | tf_op jit(solution)/shard_map/ppermute | solution.py:231
  61.6 14.4 %all-to-all-done.wire_ref = bf16[16,104,384]{2,1,0:T(8,128)(2,1)S(1)} async-done(((bf16[16,104,384]{2,1,0:T(8,128)(2,1)}), bf16[16,104,384]{2,1,0:T(8,128)(2,1)S(1)}, u32[]{:S(2)}, u32[]{:S(2)}) %all-to-all-start) | async-done | bytes 1277984 | tf_op jit(solution)/shard_map/all_to_all | solution.py:388
  76.0 20.1 %all-gather.3.cloned.1.call-done = bf16[2048,2048]{1,0:T(8,128)(2,1)} async-done(((bf16[128,2048]{1,0:T(8,128)(2,1)}), bf16[2048,2048]{1,0:T(8,128)(2,1)}) %all-gather.3.cloned.1.call-update) | async-done | bytes 8388624 | tf_op jit(solution)/shard_map/all_gather | solution.py:384
  96.1 11.9 %experts.1 = (bf16[2,4,384,128]{3,2,1,0:T(8,128)(2,1)}, bf16[2,4,384,128]{3,2,1,0:T(8,128)(2,1)}, bf16[2,4,384,128]{3,2,1,0:T(8,128)(2,1)}, bf16[2,4,384,128]{3,...) custom-call(s32[3]{0:T(128)S(1)} %pad_add_fusion.at_ref, ...), custom_call_target="tpu_custom_call" | custom-call | flops 4000000000 | bytes 22000000 | tf_op jit(solution)/shard_map/experts/pallas_call | solution.py:293
  108.0 0.6 collective-permute-start.12
  108.6 1.5 collective-permute-start.13
  110.1 1.5 collective-permute-start.16
  111.6 1.7 collective-permute-start.17
  113.4 2.8 %copy-done = bf16[4,384,2048]{2,1,0:T(8,128)(2,1)S(1)} copy-done((bf16[4,384,2048]{2,1,0:T(8,128)(2,1)S(1)}, bf16[4,384,2048]{2,1,0:T(8,128)(2,1)}, u32[]{:S(2)}) %copy-start) | copy-done | bytes 6291480
  116.1 7.5 %hidden_grad.1 = bf16[16,96,384]{2,1,0:T(8,128)(2,1)} custom-call(s32[3]{0:T(128)S(1)} %pad_add_fusion.at_ref, bf16[4,384,2048]{2,1,0:T(8,128)(2,1)S(1)} %copy-done, bf16[4,2,128,384]{3,2,1,0:T(8,128)(2,1)} %copy-done.12, bf16[4,2,128,384]{3,2,1,0:T(8,128)(2,1)} %copy-done.15, bf16[4,2,128,384]{3,2,1,0:T(8,128)(2,1)} %copy-done.17, ...), custom_call_target="tpu_custom_call" | custom-call | flops 2400000000 | bytes 14000000 | tf_op jit(solution)/shard_map/hidden_grad/pallas_call | solution.py:317
  123.6 4.4 %all-to-all-start.1 = ((bf16[16,96,384]{2,1,0:T(8,128)(2,1)}), bf16[16,96,384]{2,1,0:T(8,128)(2,1)S(1)}, u32[]{:S(2)}, u32[]{:S(2)}) async-start(bf16[16,96,384]{2,1,0:T(8,128)(2,1)} %hidden_grad.1), calls=%async_computation.1 | async-start | bytes 2359296 | tf_op jit(solution)/shard_map/all_to_all | solution.py:394
  128.1 1.4 collective-permute-done.13.refs_2_
  129.5 1.4 fusion.1
  131.2 3.0 %collective-permute-start.14 = (bf16[4,384,128]{2,1,0:T(8,128)(2,1)S(1)}, bf16[4,384,128]{2,1,0:T(8,128)(2,1)S(1)}, u32[]{:S(2)}, u32[]{:S(2)}) collective-permute-start(bf16[4,384,128]{2,1,0:T(8,128)(2,1)S(1)} %get-tuple-element.48), channel_id=1, source_target_pairs={{0,64},{1,65},{2,66},{3,67},{4,68},{5,69},{6,70},{7,71},{8,72},{9,... | collective-permute-start | bytes 1179656 | tf_op jit(solution)/shard_map/ppermute | solution.py:231
  134.2 1.2 fusion.3
  135.5 2.8 %collective-permute-start.19 = (bf16[4,384,128]{2,1,0:T(8,128)(2,1)S(1)}, bf16[4,384,128]{2,1,0:T(8,128)(2,1)S(1)}, u32[]{:S(2)}, u32[]{:S(2)}) collective-permute-start(bf16[4,384,128]{2,1,0:T(8,128)(2,1)S(1)} %get-tuple-element.45), channel_id=1, source_target_pairs={{0,48},{1,49},{2,50},{3,51},{4,52},{5,53},{6,54},{7,55},{8,56},{9,... | collective-permute-start | bytes 1179656 | tf_op jit(solution)/shard_map/ppermute | solution.py:231
  138.3 4.1 %collective-permute-done.15.refs_4_ = bf16[4,384,128]{2,1,0:T(8,128)(2,1)S(1)} collective-permute-done((bf16[4,384,128]{2,1,0:T(8,128)(2,1)S(1)}, bf16[4,384,128]{2,1,0:T(8,128)(2,1)S(1)}, u32[]{:S(2)}, u32[]{:S(2)}) %collective-permute-start.15) | collective-permute-done | bytes 393248 | tf_op jit(solution)/shard_map/ppermute | solution.py:231
  142.3 3.2 %collective-permute-done.19.refs_9_ = bf16[4,384,128]{2,1,0:T(8,128)(2,1)S(1)} collective-permute-done((bf16[4,384,128]{2,1,0:T(8,128)(2,1)S(1)}, bf16[4,384,128]{2,1,0:T(8,128)(2,1)S(1)}, u32[]{:S(2)}, u32[]{:S(2)}) %collective-permute-start.19) | collective-permute-done | bytes 393248 | tf_op jit(solution)/shard_map/ppermute | solution.py:231
  145.5 3.4 %collective-permute-done.18.refs_8_ = bf16[4,384,128]{2,1,0:T(8,128)(2,1)S(1)} collective-permute-done((bf16[4,384,128]{2,1,0:T(8,128)(2,1)S(1)}, bf16[4,384,128]{2,1,0:T(8,128)(2,1)S(1)}, u32[]{:S(2)}, u32[]{:S(2)}) %collective-permute-start.18) | collective-permute-done | bytes 393248 | tf_op jit(solution)/shard_map/ppermute | solution.py:231
  148.9 2.4 %sum_parts.1 = (bf16[2,384,128]{2,1,0:T(8,128)(2,1)S(1)}, bf16[2,384,128]{2,1,0:T(8,128)(2,1)S(1)}, bf16[2,384,128]{2,1,0:T(8,128)(2,1)}, bf16[2,384,128]{2,1,0:...) custom-call(bf16[2,4,384,128]{3,2,1,0:T(8,128)(2,1)S(1)} %copy-done., ...), custom_call_target="tpu_custom_call" | custom-call | flops 6000000000 | bytes 4000000 | tf_op jit(solution)/shard_map/sum_parts/pallas_call | solution.py:339
  151.4 0.7 copy-done.1
  152.1 0.7 copy-done.3
  152.7 1.8 collective-permute-start.21
  154.5 1.5 collective-permute-start.22
  156.3 0.9 collective-permute-start.24
  157.2 5.2 %collective-permute-done.20.refs_1_ = bf16[2,384,128]{2,1,0:T(8,128)(2,1)S(1)} collective-permute-done((bf16[2,384,128]{2,1,0:T(8,128)(2,1)S(1)}, bf16[2,384,128]{2,1,0:T(8,128)(2,1)S(1)}, u32[]{:S(2)}, u32[]{:S(2)}) %collective-permute-start.20) | collective-permute-done | bytes 196640 | tf_op jit(solution)/shard_map/ppermute | solution.py:231
  162.4 1.1 copy-done.7
  163.6 3.1 %unpack.1 = (bf16[1024,384]{1,0:T(8,128)(2,1)}, bf16[8,128]{1,0:T(8,128)(2,1)}) custom-call(s32[8,128]{1,0:T(8,128)S(1)} %bitcast.36, f32[8,128]{1,0:T(8,128)S(1)} %get-tuple-element.24.pos_ref, bf16[8,128]{1,0:T(8,128)(2,1)S(1)} %bitcast.38, bf16[1024,384]{1,0:T(8,128)(2,1)S(1)} %bitcast.34, bf16[1536,384]{1,0:T(8,128)(2,1)S(1)} %bitcast.31), custom_call_target="tpu_custom_call" | custom-call | flops 1207959552 | bytes 4194304 | tf_op jit(solution)/shard_map/unpack/pallas_call | solution.py:352
  166.7 2.8 %collective-permute-done.25.refs_7_ = bf16[2,384,128]{2,1,0:T(8,128)(2,1)S(1)} collective-permute-done((bf16[2,384,128]{2,1,0:T(8,128)(2,1)}, bf16[2,384,128]{2,1,0:T(8,128)(2,1)S(1)}, u32[]{:S(2)}, u32[]{:S(2)}) %collective-permute-start.25) | collective-permute-done | bytes 196640 | tf_op jit(solution)/shard_map/ppermute | solution.py:231
  169.5 0.7 copy-done.5
  170.2 1.2 finish.1
  (62 shorter events, 2.1 us)
Async XLA Ops:
  7.2 12.9 %copy-start.8 = (s32[128,8]{0,1:T(8,128)S(1)}, s32[128,8]{0,1:T(8,128)}, u32[]{:S(2)}) copy-start(s32[128,8]{0,1:T(8,128)} %param.8) | copy-start | bytes 12292
  7.2 12.9 %copy-start.9 = (bf16[128,8]{0,1:T(8,128)(2,1)S(1)}, bf16[128,8]{0,1:T(8,128)(2,1)}, u32[]{:S(2)}) copy-start(bf16[128,8]{0,1:T(8,128)(2,1)} %param.7) | copy-start | bytes 6148
  7.2 12.9 %copy-start.6 = (bf16[128,8,384]{2,1,0:T(8,128)(2,1)S(1)}, bf16[128,8,384]{2,1,0:T(8,128)(2,1)}, u32[]{:S(2)}) copy-start(bf16[128,8,384]{2,1,0:T(8,128)(2,1)} %param.6) | copy-start | bytes 2359300
  7.2 88.9 %all-gather.3.cloned.1.call-start = ((), (), s32[]{:S(2)}) async-start(), calls=%async_computation.2 | async-start | bytes 8912896 | tf_op jit(solution)/shard_map/all_gather | solution.py:384
  9.1 9.4 %collective-permute-start.1 = (bf16[2,128,384]{2,1,0:T(8,128)(2,1)S(1)}, bf16[2,128,384]{2,1,0:T(8,128)(2,1)S(1)}, u32[]{:S(2)}, u32[]{:S(2)}) collective-permute-start(bf16[2,128,384]{2,1,0:T(8,128)(2,1)S(1)} %get-tuple-element.52), channel_id=1, source_target_pairs={{0,128},{1,129},{2,130},{3,131},{4,132},{5,133},{6,134},{7,135},{8... | collective-permute-start | bytes 589832 | tf_op jit(solution)/shard_map/ppermute | solution.py:231
  10.6 21.2 %collective-permute-start = (bf16[2,128,384]{2,1,0:T(8,128)(2,1)S(1)}, bf16[2,128,384]{2,1,0:T(8,128)(2,1)S(1)}, u32[]{:S(2)}, u32[]{:S(2)}) collective-permute-start(bf16[2,128,384]{2,1,0:T(8,128)(2,1)S(1)} %get-tuple-element.52), channel_id=1, source_target_pairs={{0,192},{1,193},{2,194},{3,195},{4,196},{5,197},{6,198},{7,199},{8... | collective-permute-start | bytes 589832 | tf_op jit(solution)/shard_map/ppermute | solution.py:231
  12.2 19.6 %collective-permute-start.2 = (bf16[2,128,384]{2,1,0:T(8,128)(2,1)S(1)}, bf16[2,128,384]{2,1,0:T(8,128)(2,1)S(1)}, u32[]{:S(2)}, u32[]{:S(2)}) collective-permute-start(bf16[2,128,384]{2,1,0:T(8,128)(2,1)S(1)} %get-tuple-element.52), channel_id=1, source_target_pairs={{0,64},{1,65},{2,66},{3,67},{4,68},{5,69},{6,70},{7,71},{8,72},{9,... | collective-permute-start | bytes 589832 | tf_op jit(solution)/shard_map/ppermute | solution.py:231
  13.8 20.6 %collective-permute-start.7 = (bf16[2,128,384]{2,1,0:T(8,128)(2,1)S(1)}, bf16[2,128,384]{2,1,0:T(8,128)(2,1)S(1)}, u32[]{:S(2)}, u32[]{:S(2)}) collective-permute-start(bf16[2,128,384]{2,1,0:T(8,128)(2,1)S(1)} %get-tuple-element.51), channel_id=1, source_target_pairs={{0,32},{1,33},{2,34},{3,35},{4,36},{5,37},{6,38},{7,39},{8,40},{9,... | collective-permute-start | bytes 589832 | tf_op jit(solution)/shard_map/ppermute | solution.py:231
  17.0 17.4 %collective-permute-start.6 = (bf16[2,128,384]{2,1,0:T(8,128)(2,1)S(1)}, bf16[2,128,384]{2,1,0:T(8,128)(2,1)S(1)}, u32[]{:S(2)}, u32[]{:S(2)}) collective-permute-start(bf16[2,128,384]{2,1,0:T(8,128)(2,1)S(1)} %get-tuple-element.51), channel_id=1, source_target_pairs={{0,48},{1,49},{2,50},{3,51},{4,52},{5,53},{6,54},{7,55},{8,56},{9,... | collective-permute-start | bytes 589832 | tf_op jit(solution)/shard_map/ppermute | solution.py:231
  18.5 15.9 %collective-permute-start.8 = (bf16[2,128,384]{2,1,0:T(8,128)(2,1)S(1)}, bf16[2,128,384]{2,1,0:T(8,128)(2,1)S(1)}, u32[]{:S(2)}, u32[]{:S(2)}) collective-permute-start(bf16[2,128,384]{2,1,0:T(8,128)(2,1)S(1)} %get-tuple-element.51), channel_id=1, source_target_pairs={{0,16},{1,17},{2,18},{3,19},{4,20},{5,21},{6,22},{7,23},{8,24},{9,... | collective-permute-start | bytes 589832 | tf_op jit(solution)/shard_map/ppermute | solution.py:231
  23.2 52.8 %all-to-all-start = ((bf16[16,104,384]{2,1,0:T(8,128)(2,1)}), bf16[16,104,384]{2,1,0:T(8,128)(2,1)S(1)}, u32[]{:S(2)}, u32[]{:S(2)}) async-start(bf16[16,104,384]{2,1,0:T(8,128)(2,1)} %get-tuple-element.25), calls=%async_computation | async-start | bytes 2555904 | tf_op jit(solution)/shard_map/all_to_all | solution.py:388
  31.9 0.9 copy-start.12
  32.8 13.2 %collective-permute-start.3 = (bf16[4,2,128,384]{3,2,1,0:T(8,128)(2,1)S(1)}, bf16[4,2,128,384]{3,2,1,0:T(8,128)(2,1)S(1)}, u32[]{:S(2)}, u32[]{:S(2)}) collective-permute-start(bf16[4,2,128,384]{3,2,1,0:T(8,128)(2,1)S(1)} %pad_maximum_fusion.refs_0_), channel_id=1, source_target_pairs={{0,16},{1,49},{2,18},{3,51},{4,20},{5,53},{6,22},{7,55},{8,24},{9,... | collective-permute-start | bytes 2359304 | tf_op jit(solution)/shard_map/ppermute | solution.py:231
  34.5 11.5 %copy-start.13 = (bf16[4,2,128,384]{3,2,1,0:T(8,128)(2,1)}, bf16[4,2,128,384]{3,2,1,0:T(8,128)(2,1)S(1)}, u32[]{:S(2)}) copy-start(bf16[4,2,128,384]{3,2,1,0:T(8,128)(2,1)S(1)} %pad_maximum_fusion.1.refs_4_) | copy-start | bytes 2359300
  34.6 12.1 %collective-permute-start.9 = (bf16[4,2,128,384]{3,2,1,0:T(8,128)(2,1)S(1)}, bf16[4,2,128,384]{3,2,1,0:T(8,128)(2,1)S(1)}, u32[]{:S(2)}, u32[]{:S(2)}) collective-permute-start(bf16[4,2,128,384]{3,2,1,0:T(8,128)(2,1)S(1)} %pad_maximum_fusion.1.refs_4_), channel_id=1, source_target_pairs={{0,64},{1,193},{2,66},{3,195},{4,68},{5,197},{6,70},{7,199},{8,72}... | collective-permute-start | bytes 2359304 | tf_op jit(solution)/shard_map/ppermute | solution.py:231
  46.0 0.9 copy-start.15
  46.0 13.2 %collective-permute-start.4 = (bf16[4,2,128,384]{3,2,1,0:T(8,128)(2,1)S(1)}, bf16[4,2,128,384]{3,2,1,0:T(8,128)(2,1)S(1)}, u32[]{:S(2)}, u32[]{:S(2)}) collective-permute-start(bf16[4,2,128,384]{3,2,1,0:T(8,128)(2,1)S(1)} %collective-permute-done.3.refs_1_), channel_id=1, source_target_pairs={{0,16},{1,49},{2,18},{3,51},{4,20},{5,53},{6,22},{7,55},{8,24},{9,... | collective-permute-start | bytes 2359304 | tf_op jit(solution)/shard_map/ppermute | solution.py:231
  47.0 12.3 %copy-start.16 = (bf16[4,2,128,384]{3,2,1,0:T(8,128)(2,1)}, bf16[4,2,128,384]{3,2,1,0:T(8,128)(2,1)S(1)}, u32[]{:S(2)}) copy-start(bf16[4,2,128,384]{3,2,1,0:T(8,128)(2,1)S(1)} %collective-permute-done.9.refs_5_) | copy-start | bytes 2359300
  47.0 12.3 %collective-permute-start.10 = (bf16[4,2,128,384]{3,2,1,0:T(8,128)(2,1)S(1)}, bf16[4,2,128,384]{3,2,1,0:T(8,128)(2,1)S(1)}, u32[]{:S(2)}, u32[]{:S(2)}) collective-permute-start(bf16[4,2,128,384]{3,2,1,0:T(8,128)(2,1)S(1)} %collective-permute-done.9.refs_5_), channel_id=1, source_target_pairs={{0,64},{1,193},{2,66},{3,195},{4,68},{5,197},{6,70},{7,199},{8,72}... | collective-permute-start | bytes 2359304 | tf_op jit(solution)/shard_map/ppermute | solution.py:231
  59.2 48.8 %copy-start.17 = (bf16[4,2,128,384]{3,2,1,0:T(8,128)(2,1)}, bf16[4,2,128,384]{3,2,1,0:T(8,128)(2,1)S(1)}, u32[]{:S(2)}) copy-start(bf16[4,2,128,384]{3,2,1,0:T(8,128)(2,1)S(1)} %collective-permute-done.4.refs_2_) | copy-start | bytes 2359300
  59.2 16.8 %collective-permute-start.5 = (bf16[4,2,128,384]{3,2,1,0:T(8,128)(2,1)S(1)}, bf16[4,2,128,384]{3,2,1,0:T(8,128)(2,1)}, u32[]{:S(2)}, u32[]{:S(2)}) collective-permute-start(bf16[4,2,128,384]{3,2,1,0:T(8,128)(2,1)S(1)} %collective-permute-done.4.refs_2_), channel_id=1, source_target_pairs={{0,16},{1,49},{2,18},{3,51},{4,20},{5,53},{6,22},{7,55},{8,24},{9,... | collective-permute-start | bytes 2359304 | tf_op jit(solution)/shard_map/ppermute | solution.py:231
  59.2 48.8 %copy-start.18 = (bf16[4,2,128,384]{3,2,1,0:T(8,128)(2,1)}, bf16[4,2,128,384]{3,2,1,0:T(8,128)(2,1)S(1)}, u32[]{:S(2)}) copy-start(bf16[4,2,128,384]{3,2,1,0:T(8,128)(2,1)S(1)} %collective-permute-done.10.refs_6_) | copy-start | bytes 2359300
  59.3 16.7 %collective-permute-start.11 = (bf16[4,2,128,384]{3,2,1,0:T(8,128)(2,1)S(1)}, bf16[4,2,128,384]{3,2,1,0:T(8,128)(2,1)}, u32[]{:S(2)}, u32[]{:S(2)}) collective-permute-start(bf16[4,2,128,384]{3,2,1,0:T(8,128)(2,1)S(1)} %collective-permute-done.10.refs_6_), channel_id=1, source_target_pairs={{0,64},{1,193},{2,66},{3,195},{4,68},{5,197},{6,70},{7,199},{8,72}... | collective-permute-start | bytes 2359304 | tf_op jit(solution)/shard_map/ppermute | solution.py:231
  108.0 20.1 %collective-permute-start.12 = (bf16[2,4,384,128]{3,2,1,0:T(8,128)(2,1)}, bf16[2,4,384,128]{3,2,1,0:T(8,128)(2,1)S(1)}, u32[]{:S(2)}, u32[]{:S(2)}) collective-permute-start(bf16[2,4,384,128]{3,2,1,0:T(8,128)(2,1)} %get-tuple-element.30), channel_id=1, source_target_pairs={{0,64},{1,65},{2,66},{3,67},{4,68},{5,69},{6,70},{7,71},{8,72},{9,... | collective-permute-start | bytes 2359304 | tf_op jit(solution)/shard_map/ppermute | solution.py:231
  108.6 20.8 %collective-permute-start.13 = (bf16[2,4,384,128]{3,2,1,0:T(8,128)(2,1)}, bf16[2,4,384,128]{3,2,1,0:T(8,128)(2,1)S(1)}, u32[]{:S(2)}, u32[]{:S(2)}) collective-permute-start(bf16[2,4,384,128]{3,2,1,0:T(8,128)(2,1)} %get-tuple-element.31), channel_id=1, source_target_pairs={{0,192},{1,193},{2,194},{3,195},{4,196},{5,197},{6,198},{7,199},{8... | collective-permute-start | bytes 2359304 | tf_op jit(solution)/shard_map/ppermute | solution.py:231
  110.1 24.1 %collective-permute-start.16 = (bf16[2,4,384,128]{3,2,1,0:T(8,128)(2,1)}, bf16[2,4,384,128]{3,2,1,0:T(8,128)(2,1)S(1)}, u32[]{:S(2)}, u32[]{:S(2)}) collective-permute-start(bf16[2,4,384,128]{3,2,1,0:T(8,128)(2,1)} %get-tuple-element.34), channel_id=1, source_target_pairs={{0,16},{1,17},{2,18},{3,19},{4,20},{5,21},{6,22},{7,23},{8,24},{9,... | collective-permute-start | bytes 2359304 | tf_op jit(solution)/shard_map/ppermute | solution.py:231
  111.6 22.6 %collective-permute-start.17 = (bf16[2,4,384,128]{3,2,1,0:T(8,128)(2,1)}, bf16[2,4,384,128]{3,2,1,0:T(8,128)(2,1)}, u32[]{:S(2)}, u32[]{:S(2)}) collective-permute-start(bf16[2,4,384,128]{3,2,1,0:T(8,128)(2,1)} %get-tuple-element.35), channel_id=1, source_target_pairs={{0,48},{1,49},{2,50},{3,51},{4,52},{5,53},{6,54},{7,55},{8,56},{9,... | collective-permute-start | bytes 2359304 | tf_op jit(solution)/shard_map/ppermute | solution.py:231
  113.3 2.8 %copy-start = (bf16[4,384,2048]{2,1,0:T(8,128)(2,1)S(1)}, bf16[4,384,2048]{2,1,0:T(8,128)(2,1)}, u32[]{:S(2)}) copy-start(bf16[4,384,2048]{2,1,0:T(8,128)(2,1)} %get-tuple-element.26.x_hbm) | copy-start | bytes 18874372
  123.6 38.8 %all-to-all-start.1 = ((bf16[16,96,384]{2,1,0:T(8,128)(2,1)}), bf16[16,96,384]{2,1,0:T(8,128)(2,1)S(1)}, u32[]{:S(2)}, u32[]{:S(2)}) async-start(bf16[16,96,384]{2,1,0:T(8,128)(2,1)} %hidden_grad.1), calls=%async_computation.1 | async-start | bytes 2359296 | tf_op jit(solution)/shard_map/all_to_all | solution.py:394
  128.1 6.1 %copy-start.14 = (bf16[2,4,384,128]{3,2,1,0:T(8,128)(2,1)S(1)}, bf16[2,4,384,128]{3,2,1,0:T(8,128)(2,1)}, u32[]{:S(2)}) copy-start(bf16[2,4,384,128]{3,2,1,0:T(8,128)(2,1)} %get-tuple-element.36) | copy-start | bytes 2359300
  130.9 18.1 %copy-start.10 = (bf16[2,4,384,128]{3,2,1,0:T(8,128)(2,1)S(1)}, bf16[2,4,384,128]{3,2,1,0:T(8,128)(2,1)}, u32[]{:S(2)}) copy-start(bf16[2,4,384,128]{3,2,1,0:T(8,128)(2,1)} %get-tuple-element.29.refs_0_) | copy-start | bytes 2359300
  130.9 18.1 %copy-start.11 = (bf16[2,4,384,128]{3,2,1,0:T(8,128)(2,1)S(1)}, bf16[2,4,384,128]{3,2,1,0:T(8,128)(2,1)}, u32[]{:S(2)}) copy-start(bf16[2,4,384,128]{3,2,1,0:T(8,128)(2,1)} %get-tuple-element.33.refs_5_) | copy-start | bytes 2359300
  130.9 11.5 %collective-permute-start.15 = (bf16[4,384,128]{2,1,0:T(8,128)(2,1)S(1)}, bf16[4,384,128]{2,1,0:T(8,128)(2,1)S(1)}, u32[]{:S(2)}, u32[]{:S(2)}) collective-permute-start(bf16[4,384,128]{2,1,0:T(8,128)(2,1)S(1)} %get-tuple-element.47), channel_id=1, source_target_pairs={{0,192},{1,193},{2,194},{3,195},{4,196},{5,197},{6,198},{7,199},{8... | collective-permute-start | bytes 1179656 | tf_op jit(solution)/shard_map/ppermute | solution.py:231
  131.2 11.1 %collective-permute-start.14 = (bf16[4,384,128]{2,1,0:T(8,128)(2,1)S(1)}, bf16[4,384,128]{2,1,0:T(8,128)(2,1)S(1)}, u32[]{:S(2)}, u32[]{:S(2)}) collective-permute-start(bf16[4,384,128]{2,1,0:T(8,128)(2,1)S(1)} %get-tuple-element.48), channel_id=1, source_target_pairs={{0,64},{1,65},{2,66},{3,67},{4,68},{5,69},{6,70},{7,71},{8,72},{9,... | collective-permute-start | bytes 1179656 | tf_op jit(solution)/shard_map/ppermute | solution.py:231
  135.5 10.0 %collective-permute-start.19 = (bf16[4,384,128]{2,1,0:T(8,128)(2,1)S(1)}, bf16[4,384,128]{2,1,0:T(8,128)(2,1)S(1)}, u32[]{:S(2)}, u32[]{:S(2)}) collective-permute-start(bf16[4,384,128]{2,1,0:T(8,128)(2,1)S(1)} %get-tuple-element.45), channel_id=1, source_target_pairs={{0,48},{1,49},{2,50},{3,51},{4,52},{5,53},{6,54},{7,55},{8,56},{9,... | collective-permute-start | bytes 1179656 | tf_op jit(solution)/shard_map/ppermute | solution.py:231
  138.3 10.6 %collective-permute-start.18 = (bf16[4,384,128]{2,1,0:T(8,128)(2,1)S(1)}, bf16[4,384,128]{2,1,0:T(8,128)(2,1)S(1)}, u32[]{:S(2)}, u32[]{:S(2)}) collective-permute-start(bf16[4,384,128]{2,1,0:T(8,128)(2,1)S(1)} %get-tuple-element.46), channel_id=1, source_target_pairs={{0,16},{1,17},{2,18},{3,19},{4,20},{5,21},{6,22},{7,23},{8,24},{9,... | collective-permute-start | bytes 1179656 | tf_op jit(solution)/shard_map/ppermute | solution.py:231
  151.4 0.7 copy-start.1
  152.0 0.7 copy-start.3
  152.7 9.7 %collective-permute-start.20 = (bf16[2,384,128]{2,1,0:T(8,128)(2,1)S(1)}, bf16[2,384,128]{2,1,0:T(8,128)(2,1)S(1)}, u32[]{:S(2)}, u32[]{:S(2)}) collective-permute-start(bf16[2,384,128]{2,1,0:T(8,128)(2,1)S(1)} %get-tuple-element.38), channel_id=1, source_target_pairs={{0,16},{1,17},{2,18},{3,19},{4,20},{5,21},{6,22},{7,23},{8,24},{9,... | collective-permute-start | bytes 589832 | tf_op jit(solution)/shard_map/ppermute | solution.py:231
  152.7 14.0 %collective-permute-start.21 = (bf16[2,384,128]{2,1,0:T(8,128)(2,1)}, bf16[2,384,128]{2,1,0:T(8,128)(2,1)S(1)}, u32[]{:S(2)}, u32[]{:S(2)}) collective-permute-start(bf16[2,384,128]{2,1,0:T(8,128)(2,1)} %get-tuple-element.39), channel_id=1, source_target_pairs={{0,32},{1,33},{2,34},{3,35},{4,36},{5,37},{6,38},{7,39},{8,40},{9,... | collective-permute-start | bytes 589832 | tf_op jit(solution)/shard_map/ppermute | solution.py:231
  154.5 12.2 %collective-permute-start.22 = (bf16[2,384,128]{2,1,0:T(8,128)(2,1)}, bf16[2,384,128]{2,1,0:T(8,128)(2,1)S(1)}, u32[]{:S(2)}, u32[]{:S(2)}) collective-permute-start(bf16[2,384,128]{2,1,0:T(8,128)(2,1)} %get-tuple-element.40), channel_id=1, source_target_pairs={{0,48},{1,49},{2,50},{3,51},{4,52},{5,53},{6,54},{7,55},{8,56},{9,... | collective-permute-start | bytes 589832 | tf_op jit(solution)/shard_map/ppermute | solution.py:231
  156.0 10.8 %collective-permute-start.23 = (bf16[2,384,128]{2,1,0:T(8,128)(2,1)}, bf16[2,384,128]{2,1,0:T(8,128)(2,1)S(1)}, u32[]{:S(2)}, u32[]{:S(2)}) collective-permute-start(bf16[2,384,128]{2,1,0:T(8,128)(2,1)} %get-tuple-element.42), channel_id=1, source_target_pairs={{0,64},{1,65},{2,66},{3,67},{4,68},{5,69},{6,70},{7,71},{8,72},{9,... | collective-permute-start | bytes 589832 | tf_op jit(solution)/shard_map/ppermute | solution.py:231
  156.3 10.5 %collective-permute-start.24 = (bf16[2,384,128]{2,1,0:T(8,128)(2,1)}, bf16[2,384,128]{2,1,0:T(8,128)(2,1)S(1)}, u32[]{:S(2)}, u32[]{:S(2)}) collective-permute-start(bf16[2,384,128]{2,1,0:T(8,128)(2,1)} %get-tuple-element.43), channel_id=1, source_target_pairs={{0,128},{1,129},{2,130},{3,131},{4,132},{5,133},{6,134},{7,135},{8... | collective-permute-start | bytes 589832 | tf_op jit(solution)/shard_map/ppermute | solution.py:231
  162.4 7.1 %collective-permute-start.25 = (bf16[2,384,128]{2,1,0:T(8,128)(2,1)}, bf16[2,384,128]{2,1,0:T(8,128)(2,1)S(1)}, u32[]{:S(2)}, u32[]{:S(2)}) collective-permute-start(bf16[2,384,128]{2,1,0:T(8,128)(2,1)} %get-tuple-element.44), channel_id=1, source_target_pairs={{0,192},{1,193},{2,194},{3,195},{4,196},{5,197},{6,198},{7,199},{8... | collective-permute-start | bytes 589832 | tf_op jit(solution)/shard_map/ppermute | solution.py:231
  162.4 1.1 copy-start.7
  163.6 6.0 %copy-start.2 = (bf16[2,384,128]{2,1,0:T(8,128)(2,1)S(1)}, bf16[2,384,128]{2,1,0:T(8,128)(2,1)}, u32[]{:S(2)}) copy-start(bf16[2,384,128]{2,1,0:T(8,128)(2,1)} %copy-done.1) | copy-start | bytes 589828
  163.6 6.0 %copy-start.4 = (bf16[2,384,128]{2,1,0:T(8,128)(2,1)S(1)}, bf16[2,384,128]{2,1,0:T(8,128)(2,1)}, u32[]{:S(2)}) copy-start(bf16[2,384,128]{2,1,0:T(8,128)(2,1)} %copy-done.3) | copy-start | bytes 589828
  169.5 0.7 copy-start.5
Sparse Core Ops, SparseCore 0:
  9.9 86.1 all-gather.2

commit v3 on v2

--- a/solution.py
+++ b/solution.py
@@ -202,12 +202,24 @@
 
 
 def sum_kernel(*refs):
+    kept, sem = refs[10 + 2 * SIDE :]
+    copies = []
     for h in range(2):
         own, on, back, on_later, back_later = refs[5 * h : 5 * h + 5]
         outs = refs[10 + SIDE * h : 10 + SIDE * (h + 1)]
         for d in range(SIDE):
-            outs[d][0] = add(own[0, d], back[1, d], on_later[d]).astype(BF16)
-            outs[d][1] = add(own[1, d], on[1, d], back_later[d]).astype(BF16)
+            first = add(own[0, d], back[1, d], on_later[d]).astype(BF16)
+            second = add(own[1, d], on[1, d], back_later[d]).astype(BF16)
+            if d == 0:
+                kept[h, 0] = first
+                kept[h, 1] = second
+                copies.append(pltpu.make_async_copy(kept.at[h], outs[0], sem.at[h]))
+                copies[-1].start()
+            else:
+                outs[d][0] = first
+                outs[d][1] = second
+    for c in copies:
+        c.wait()
 
 
 def finish_kernel(after_ref, *refs):
@@ -331,16 +343,17 @@
         compiler_params=params(28),
         cost_estimate=cost(HIDDEN_FLOPS, 14e6),
         name="hidden_grad",
-    )(at, x, *pieces)
+    )(at, pltpu.with_memory_space_constraint(x, pltpu.HBM), *pieces)
 
 
 def sum_call(parts):
     _, _, width, depth = parts[0].shape
     return pl.pallas_call(
         sum_kernel,
-        out_shape=[sds((2, width, depth), BF16)] * (2 * SIDE),
+        out_shape=([pltpu.HBM((2, width, depth), BF16)] + [sds((2, width, depth), BF16)] * (SIDE - 1)) * 2,
         in_specs=[VMEM] * len(parts),
-        out_specs=[VMEM] * (2 * SIDE),
+        out_specs=([HBM] + [VMEM] * (SIDE - 1)) * 2,
+        scratch_shapes=[pltpu.VMEM((2, 2, width, depth), BF16), pltpu.SemaphoreType.DMA((2,))],
         compiler_params=params(24),
         cost_estimate=cost(SUM_FLOPS, 4e6),
         name="sum_parts",
@@ -364,12 +377,12 @@
     return pl.pallas_call(
         finish_kernel,
         out_shape=sds((depth, local, width), F32),
-        in_specs=[ANY] + [VMEM] * len(parts),
+        in_specs=[HBM] + [VMEM] * len(parts),
         out_specs=VMEM,
         compiler_params=params(12),
         cost_estimate=cost(2**20, 2.5e6),
         name="finish",
-    )(after, *parts)
+    )(pltpu.with_memory_space_constraint(after, pltpu.HBM), *parts)
 
 
 def per_device(out_grad, saved_hidden, gate_weight, expert_ids, down_weight):

time: 179 us -> 177 us (0.989)
  local copies, waits for them, and re-layouts: 8.36 us -> 3.5 us
  waiting for transfers between devices: 77.9 us -> 80.2 us
    unnamed x39 -> x31, local copies, waits for them, and re-layouts: 8.28 us -> 3.43 us
    ppermute x26, waiting for transfers between devices: 42.6 us -> 45 us  [shift(): return lax.ppermute(x, ('dp', 'expert'), pairs)]
  transfers between devices with their start and end apart: 29 -> 29, of which waited for: 12 -> 13; matrix products, arithmetic and copies ran while one was open for 2% -> 2% of each run, Pallas kernels for 9% -> 10%
where the time goes in v3:
time: 177 us
  waiting for transfers between devices  80.2 us (45%)
  starting transfers between devices  45.8 us (26%)
  Pallas kernels  30.3 us (17%)
  between operations  14.3 us (8%)
  local copies, waits for them, and re-layouts  3.5 us (2%)
  other arithmetic  2.96 us (2%)
    ppermute x26, waiting for transfers between devices, shift(): return lax.ppermute(x, ('dp', 'expert'), pairs)  45 us
    ppermute x26, starting transfers between devices, shift(): return lax.ppermute(x, ('dp', 'expert'), pairs)  32.8 us
    all_gather x1, waiting for transfers between devices, per_device(): grads = lax.all_gather(out_grad, 'expert', axis=0, tiled=False)  20.1 us
    all_to_all x1, waiting for transfers between devices, per_device(): lax.all_to_all(wire, 'expert', split_axis=0, concat_axis=0, tiled=True)  14.4 us
    pallas_call x1, Pallas kernels, expert_call(): pl.pallas_call(functools.partial(expert_kernel, local), out_shape=[pltpu....  11.9 us
    all_to_all x1, starting transfers between devices, per_device(): lax.all_to_all(wire, 'expert', split_axis=0, concat_axis=0, tiled=True)  8.57 us
    pallas_call x1, Pallas kernels, hidden_call(): pl.pallas_call(functools.partial(hidden_kernel, local), out_shape=pltpu.H...  8 us
    all_to_all x1, starting transfers between devices, per_device(): back = lax.all_to_all(u, 'expert', split_axis=0, concat_axis=0, tiled=True)  4.4 us
  transfers between devices with their start and end apart: 29, of which 13 were waited for; matrix products, arithmetic and copies ran while one was open for 2% of the time, Pallas kernels for 10%

profile of v3, /device:TPU:6, one launch (start us, length us, event | category | flops | bytes accessed | tf_op | source)
XLA Modules:
  0.0 177.0 jit_solution(5223681103975950228)
XLA Ops:
  7.2 0.7 all-gather.3.cloned.1.call-update
  7.9 1.0 copy.10
  9.1 1.5 collective-permute-start.1
  10.6 1.7 collective-permute-start
  12.2 1.6 collective-permute-start.2
  13.8 3.2 %collective-permute-start.7 = (bf16[2,128,384]{2,1,0:T(8,128)(2,1)S(1)}, bf16[2,128,384]{2,1,0:T(8,128)(2,1)S(1)}, u32[]{:S(2)}, u32[]{:S(2)}) collective-permute-start(bf16[2,128,384]{2,1,0:T(8,128)(2,1)S(1)} %get-tuple-element.51), channel_id=1, source_target_pairs={{0,32},{1,33},{2,34},{3,35},{4,36},{5,37},{6,38},{7,39},{8,40},{9,... | collective-permute-start | bytes 589832 | tf_op jit(solution)/shard_map/ppermute | solution.py:243
  17.0 1.1 collective-permute-start.6
  18.0 0.4 collective-permute-done.1
  18.5 1.6 collective-permute-start.8
  20.1 3.1 %pack.1 = (bf16[16,104,384]{2,1,0:T(8,128)(2,1)}, f32[8,128]{1,0:T(8,128)S(1)}) custom-call(s32[8,128]{1,0:T(8,128)S(1)} %bitcast.34, bf16[8,128]{1,0:T(8,128)(2,1)S(1)} %bitcast.36, bf16[1024,384]{1,0:T(8,128)(2,1)S(1)} %bitcast.32), custom_call_target="tpu_custom_call" | custom-call | flops 1207959552 | bytes 4194304 | tf_op jit(solution)/shard_map/pack/pallas_call | solution.py:289
  23.2 8.6 %all-to-all-start = ((bf16[16,104,384]{2,1,0:T(8,128)(2,1)}), bf16[16,104,384]{2,1,0:T(8,128)(2,1)S(1)}, u32[]{:S(2)}, u32[]{:S(2)}) async-start(bf16[16,104,384]{2,1,0:T(8,128)(2,1)} %get-tuple-element.25), calls=%async_computation | async-start | bytes 2555904 | tf_op jit(solution)/shard_map/all_to_all | solution.py:401
  31.9 0.9 copy-done.8
  32.8 1.6 collective-permute-start.3
  34.5 0.5 collective-permute-start.9
  35.1 11.0 %collective-permute-done.3.refs_1_ = bf16[4,2,128,384]{3,2,1,0:T(8,128)(2,1)S(1)} collective-permute-done((bf16[4,2,128,384]{3,2,1,0:T(8,128)(2,1)S(1)}, bf16[4,2,128,384]{3,2,1,0:T(8,128)(2,1)S(1)}, u32[]{:S(2)}, u32[]{:S(2)}) %collective-permute-start.3) | collective-permute-done | bytes 786464 | tf_op jit(solution)/shard_map/ppermute | solution.py:243
  46.0 0.4 collective-permute-start.4
  46.6 0.3 copy-done.11
  46.9 1.3 collective-permute-start.10
  48.3 11.0 %collective-permute-done.4.refs_2_ = bf16[4,2,128,384]{3,2,1,0:T(8,128)(2,1)S(1)} collective-permute-done((bf16[4,2,128,384]{3,2,1,0:T(8,128)(2,1)S(1)}, bf16[4,2,128,384]{3,2,1,0:T(8,128)(2,1)S(1)}, u32[]{:S(2)}, u32[]{:S(2)}) %collective-permute-start.4) | collective-permute-done | bytes 786464 | tf_op jit(solution)/shard_map/ppermute | solution.py:243
  59.3 2.2 %collective-permute-start.11 = (bf16[4,2,128,384]{3,2,1,0:T(8,128)(2,1)S(1)}, bf16[4,2,128,384]{3,2,1,0:T(8,128)(2,1)}, u32[]{:S(2)}, u32[]{:S(2)}) collective-permute-start(bf16[4,2,128,384]{3,2,1,0:T(8,128)(2,1)S(1)} %collective-permute-done.10.refs_6_), channel_id=1, source_target_pairs={{0,64},{1,193},{2,66},{3,195},{4,68},{5,197},{6,70},{7,199},{8,72}... | collective-permute-start | bytes 2359304 | tf_op jit(solution)/shard_map/ppermute | solution.py:243
  61.5 14.4 %all-to-all-done.wire_ref = bf16[16,104,384]{2,1,0:T(8,128)(2,1)S(1)} async-done(((bf16[16,104,384]{2,1,0:T(8,128)(2,1)}), bf16[16,104,384]{2,1,0:T(8,128)(2,1)S(1)}, u32[]{:S(2)}, u32[]{:S(2)}) %all-to-all-start) | async-done | bytes 1277984 | tf_op jit(solution)/shard_map/all_to_all | solution.py:401
  76.0 20.1 %all-gather.3.cloned.1.call-done = bf16[2048,2048]{1,0:T(8,128)(2,1)} async-done(((bf16[128,2048]{1,0:T(8,128)(2,1)}), bf16[2048,2048]{1,0:T(8,128)(2,1)}) %all-gather.3.cloned.1.call-update) | async-done | bytes 8388624 | tf_op jit(solution)/shard_map/all_gather | solution.py:397
  96.1 11.9 %experts.1 = (bf16[2,4,384,128]{3,2,1,0:T(8,128)(2,1)}, bf16[2,4,384,128]{3,2,1,0:T(8,128)(2,1)}, bf16[2,4,384,128]{3,2,1,0:T(8,128)(2,1)}, bf16[2,4,384,128]{3,...) custom-call(s32[3]{0:T(128)S(1)} %pad_add_fusion.at_ref, ...), custom_call_target="tpu_custom_call" | custom-call | flops 4000000000 | bytes 22000000 | tf_op jit(solution)/shard_map/experts/pallas_call | solution.py:305
  108.0 0.6 collective-permute-start.12
  108.6 1.5 collective-permute-start.13
  110.1 1.5 collective-permute-start.16
  111.6 1.7 collective-permute-start.17
  113.3 8.0 %hidden_grad.1 = bf16[16,96,384]{2,1,0:T(8,128)(2,1)} custom-call(s32[3]{0:T(128)S(1)} %pad_add_fusion.at_ref, bf16[4,384,2048]{2,1,0:T(8,128)(2,1)} %get-tuple-element.26.x_hbm, bf16[4,2,128,384]{3,2,1,0:T(8,128)(2,1)} %copy-done.8, bf16[4,2,128,384]{3,2,1,0:T(8,128)(2,1)} %copy-done.11, bf16[4,2,128,384]{3,2,1,0:T(8,128)(2,1)} %copy-done.13, ...), custom_call_target="tpu_custom_call" | custom-call | flops 2400000000 | bytes 14000000 | tf_op jit(solution)/shard_map/hidden_grad/pallas_call | solution.py:329
  121.3 4.4 %all-to-all-start.1 = ((bf16[16,96,384]{2,1,0:T(8,128)(2,1)}), bf16[16,96,384]{2,1,0:T(8,128)(2,1)S(1)}, u32[]{:S(2)}, u32[]{:S(2)}) async-start(bf16[16,96,384]{2,1,0:T(8,128)(2,1)} %hidden_grad.1), calls=%async_computation.1 | async-start | bytes 2359296 | tf_op jit(solution)/shard_map/all_to_all | solution.py:407
  125.8 2.2 %collective-permute-done.12.refs_1_ = bf16[2,4,384,128]{3,2,1,0:T(8,128)(2,1)S(1)} collective-permute-done((bf16[2,4,384,128]{3,2,1,0:T(8,128)(2,1)}, bf16[2,4,384,128]{3,2,1,0:T(8,128)(2,1)S(1)}, u32[]{:S(2)}, u32[]{:S(2)}) %collective-permute-start.12) | collective-permute-done | bytes 786464 | tf_op jit(solution)/shard_map/ppermute | solution.py:243
  128.0 1.5 collective-permute-done.13.refs_2_
  129.5 1.4 fusion.1
  130.9 0.6 collective-permute-start.15
  131.4 3.0 %collective-permute-start.14 = (bf16[4,384,128]{2,1,0:T(8,128)(2,1)S(1)}, bf16[4,384,128]{2,1,0:T(8,128)(2,1)S(1)}, u32[]{:S(2)}, u32[]{:S(2)}) collective-permute-start(bf16[4,384,128]{2,1,0:T(8,128)(2,1)S(1)} %get-tuple-element.48), channel_id=1, source_target_pairs={{0,64},{1,65},{2,66},{3,67},{4,68},{5,69},{6,70},{7,71},{8,72},{9,... | collective-permute-start | bytes 1179656 | tf_op jit(solution)/shard_map/ppermute | solution.py:243
  134.4 1.2 fusion.3
  135.7 2.8 %collective-permute-start.19 = (bf16[4,384,128]{2,1,0:T(8,128)(2,1)S(1)}, bf16[4,384,128]{2,1,0:T(8,128)(2,1)S(1)}, u32[]{:S(2)}, u32[]{:S(2)}) collective-permute-start(bf16[4,384,128]{2,1,0:T(8,128)(2,1)S(1)} %get-tuple-element.45), channel_id=1, source_target_pairs={{0,48},{1,49},{2,50},{3,51},{4,52},{5,53},{6,54},{7,55},{8,56},{9,... | collective-permute-start | bytes 1179656 | tf_op jit(solution)/shard_map/ppermute | solution.py:243
  138.5 4.0 %collective-permute-done.15.refs_4_ = bf16[4,384,128]{2,1,0:T(8,128)(2,1)S(1)} collective-permute-done((bf16[4,384,128]{2,1,0:T(8,128)(2,1)S(1)}, bf16[4,384,128]{2,1,0:T(8,128)(2,1)S(1)}, u32[]{:S(2)}, u32[]{:S(2)}) %collective-permute-start.15) | collective-permute-done | bytes 393248 | tf_op jit(solution)/shard_map/ppermute | solution.py:243
  142.5 3.2 %collective-permute-done.19.refs_9_ = bf16[4,384,128]{2,1,0:T(8,128)(2,1)S(1)} collective-permute-done((bf16[4,384,128]{2,1,0:T(8,128)(2,1)S(1)}, bf16[4,384,128]{2,1,0:T(8,128)(2,1)S(1)}, u32[]{:S(2)}, u32[]{:S(2)}) %collective-permute-start.19) | collective-permute-done | bytes 393248 | tf_op jit(solution)/shard_map/ppermute | solution.py:243
  145.7 3.4 %collective-permute-done.18.refs_8_ = bf16[4,384,128]{2,1,0:T(8,128)(2,1)S(1)} collective-permute-done((bf16[4,384,128]{2,1,0:T(8,128)(2,1)S(1)}, bf16[4,384,128]{2,1,0:T(8,128)(2,1)S(1)}, u32[]{:S(2)}, u32[]{:S(2)}) %collective-permute-start.18) | collective-permute-done | bytes 393248 | tf_op jit(solution)/shard_map/ppermute | solution.py:243
  149.1 2.9 %sum_parts.1 = (bf16[2,384,128]{2,1,0:T(8,128)(2,1)}, bf16[2,384,128]{2,1,0:T(8,128)(2,1)S(1)}, bf16[2,384,128]{2,1,0:T(8,128)(2,1)}, bf16[2,384,128]{2,1,0:T(8,...) custom-call(bf16[2,4,384,128]{3,2,1,0:T(8,128)(2,1)S(1)} %copy-done., ...), custom_call_target="tpu_custom_call" | custom-call | flops 6000000000 | bytes 4000000 | tf_op jit(solution)/shard_map/sum_parts/pallas_call | solution.py:351
  152.2 1.7 collective-permute-start.21
  153.9 1.5 collective-permute-start.22
  155.7 0.9 collective-permute-start.24
  156.6 5.2 %collective-permute-done.20.refs_1_ = bf16[2,384,128]{2,1,0:T(8,128)(2,1)S(1)} collective-permute-done((bf16[2,384,128]{2,1,0:T(8,128)(2,1)S(1)}, bf16[2,384,128]{2,1,0:T(8,128)(2,1)S(1)}, u32[]{:S(2)}, u32[]{:S(2)}) %collective-permute-start.20) | collective-permute-done | bytes 196640 | tf_op jit(solution)/shard_map/ppermute | solution.py:243
  161.9 1.1 copy-done.3
  163.0 3.1 %unpack.1 = (bf16[1024,384]{1,0:T(8,128)(2,1)}, bf16[8,128]{1,0:T(8,128)(2,1)}) custom-call(s32[8,128]{1,0:T(8,128)S(1)} %bitcast.35, f32[8,128]{1,0:T(8,128)S(1)} %get-tuple-element.24.pos_ref, bf16[8,128]{1,0:T(8,128)(2,1)S(1)} %bitcast.37, bf16[1024,384]{1,0:T(8,128)(2,1)S(1)} %bitcast.33, bf16[1536,384]{1,0:T(8,128)(2,1)S(1)} %bitcast.31), custom_call_target="tpu_custom_call" | custom-call | flops 1207959552 | bytes 4194304 | tf_op jit(solution)/shard_map/unpack/pallas_call | solution.py:365
  166.2 2.8 %collective-permute-done.25.refs_7_ = bf16[2,384,128]{2,1,0:T(8,128)(2,1)S(1)} collective-permute-done((bf16[2,384,128]{2,1,0:T(8,128)(2,1)}, bf16[2,384,128]{2,1,0:T(8,128)(2,1)S(1)}, u32[]{:S(2)}, u32[]{:S(2)}) %collective-permute-start.25) | collective-permute-done | bytes 196640 | tf_op jit(solution)/shard_map/ppermute | solution.py:243
  168.9 1.2 finish.1
  (54 shorter events, 1.1 us)
Async XLA Ops:
  7.2 12.9 %copy-start.4 = (s32[128,8]{0,1:T(8,128)S(1)}, s32[128,8]{0,1:T(8,128)}, u32[]{:S(2)}) copy-start(s32[128,8]{0,1:T(8,128)} %param.8) | copy-start | bytes 12292
  7.2 12.9 %copy-start.5 = (bf16[128,8]{0,1:T(8,128)(2,1)S(1)}, bf16[128,8]{0,1:T(8,128)(2,1)}, u32[]{:S(2)}) copy-start(bf16[128,8]{0,1:T(8,128)(2,1)} %param.7) | copy-start | bytes 6148
  7.2 12.9 %copy-start.2 = (bf16[128,8,384]{2,1,0:T(8,128)(2,1)S(1)}, bf16[128,8,384]{2,1,0:T(8,128)(2,1)}, u32[]{:S(2)}) copy-start(bf16[128,8,384]{2,1,0:T(8,128)(2,1)} %param.6) | copy-start | bytes 2359300
  7.2 88.9 %all-gather.3.cloned.1.call-start = ((), (), s32[]{:S(2)}) async-start(), calls=%async_computation.2 | async-start | bytes 8912896 | tf_op jit(solution)/shard_map/all_gather | solution.py:397
  9.1 9.4 %collective-permute-start.1 = (bf16[2,128,384]{2,1,0:T(8,128)(2,1)S(1)}, bf16[2,128,384]{2,1,0:T(8,128)(2,1)S(1)}, u32[]{:S(2)}, u32[]{:S(2)}) collective-permute-start(bf16[2,128,384]{2,1,0:T(8,128)(2,1)S(1)} %get-tuple-element.52), channel_id=1, source_target_pairs={{0,128},{1,129},{2,130},{3,131},{4,132},{5,133},{6,134},{7,135},{8... | collective-permute-start | bytes 589832 | tf_op jit(solution)/shard_map/ppermute | solution.py:243
  10.6 21.2 %collective-permute-start = (bf16[2,128,384]{2,1,0:T(8,128)(2,1)S(1)}, bf16[2,128,384]{2,1,0:T(8,128)(2,1)S(1)}, u32[]{:S(2)}, u32[]{:S(2)}) collective-permute-start(bf16[2,128,384]{2,1,0:T(8,128)(2,1)S(1)} %get-tuple-element.52), channel_id=1, source_target_pairs={{0,192},{1,193},{2,194},{3,195},{4,196},{5,197},{6,198},{7,199},{8... | collective-permute-start | bytes 589832 | tf_op jit(solution)/shard_map/ppermute | solution.py:243
  12.2 19.6 %collective-permute-start.2 = (bf16[2,128,384]{2,1,0:T(8,128)(2,1)S(1)}, bf16[2,128,384]{2,1,0:T(8,128)(2,1)S(1)}, u32[]{:S(2)}, u32[]{:S(2)}) collective-permute-start(bf16[2,128,384]{2,1,0:T(8,128)(2,1)S(1)} %get-tuple-element.52), channel_id=1, source_target_pairs={{0,64},{1,65},{2,66},{3,67},{4,68},{5,69},{6,70},{7,71},{8,72},{9,... | collective-permute-start | bytes 589832 | tf_op jit(solution)/shard_map/ppermute | solution.py:243
  13.8 20.6 %collective-permute-start.7 = (bf16[2,128,384]{2,1,0:T(8,128)(2,1)S(1)}, bf16[2,128,384]{2,1,0:T(8,128)(2,1)S(1)}, u32[]{:S(2)}, u32[]{:S(2)}) collective-permute-start(bf16[2,128,384]{2,1,0:T(8,128)(2,1)S(1)} %get-tuple-element.51), channel_id=1, source_target_pairs={{0,32},{1,33},{2,34},{3,35},{4,36},{5,37},{6,38},{7,39},{8,40},{9,... | collective-permute-start | bytes 589832 | tf_op jit(solution)/shard_map/ppermute | solution.py:243
  17.0 17.4 %collective-permute-start.6 = (bf16[2,128,384]{2,1,0:T(8,128)(2,1)S(1)}, bf16[2,128,384]{2,1,0:T(8,128)(2,1)S(1)}, u32[]{:S(2)}, u32[]{:S(2)}) collective-permute-start(bf16[2,128,384]{2,1,0:T(8,128)(2,1)S(1)} %get-tuple-element.51), channel_id=1, source_target_pairs={{0,48},{1,49},{2,50},{3,51},{4,52},{5,53},{6,54},{7,55},{8,56},{9,... | collective-permute-start | bytes 589832 | tf_op jit(solution)/shard_map/ppermute | solution.py:243
  18.5 15.9 %collective-permute-start.8 = (bf16[2,128,384]{2,1,0:T(8,128)(2,1)S(1)}, bf16[2,128,384]{2,1,0:T(8,128)(2,1)S(1)}, u32[]{:S(2)}, u32[]{:S(2)}) collective-permute-start(bf16[2,128,384]{2,1,0:T(8,128)(2,1)S(1)} %get-tuple-element.51), channel_id=1, source_target_pairs={{0,16},{1,17},{2,18},{3,19},{4,20},{5,21},{6,22},{7,23},{8,24},{9,... | collective-permute-start | bytes 589832 | tf_op jit(solution)/shard_map/ppermute | solution.py:243
  23.2 52.8 %all-to-all-start = ((bf16[16,104,384]{2,1,0:T(8,128)(2,1)}), bf16[16,104,384]{2,1,0:T(8,128)(2,1)S(1)}, u32[]{:S(2)}, u32[]{:S(2)}) async-start(bf16[16,104,384]{2,1,0:T(8,128)(2,1)} %get-tuple-element.25), calls=%async_computation | async-start | bytes 2555904 | tf_op jit(solution)/shard_map/all_to_all | solution.py:401
  31.9 0.9 copy-start.8
  32.8 13.2 %collective-permute-start.3 = (bf16[4,2,128,384]{3,2,1,0:T(8,128)(2,1)S(1)}, bf16[4,2,128,384]{3,2,1,0:T(8,128)(2,1)S(1)}, u32[]{:S(2)}, u32[]{:S(2)}) collective-permute-start(bf16[4,2,128,384]{3,2,1,0:T(8,128)(2,1)S(1)} %pad_maximum_fusion.refs_0_), channel_id=1, source_target_pairs={{0,16},{1,49},{2,18},{3,51},{4,20},{5,53},{6,22},{7,55},{8,24},{9,... | collective-permute-start | bytes 2359304 | tf_op jit(solution)/shard_map/ppermute | solution.py:243
  34.5 11.5 %copy-start.9 = (bf16[4,2,128,384]{3,2,1,0:T(8,128)(2,1)}, bf16[4,2,128,384]{3,2,1,0:T(8,128)(2,1)S(1)}, u32[]{:S(2)}) copy-start(bf16[4,2,128,384]{3,2,1,0:T(8,128)(2,1)S(1)} %pad_maximum_fusion.1.refs_4_) | copy-start | bytes 2359300
  34.5 12.1 %collective-permute-start.9 = (bf16[4,2,128,384]{3,2,1,0:T(8,128)(2,1)S(1)}, bf16[4,2,128,384]{3,2,1,0:T(8,128)(2,1)S(1)}, u32[]{:S(2)}, u32[]{:S(2)}) collective-permute-start(bf16[4,2,128,384]{3,2,1,0:T(8,128)(2,1)S(1)} %pad_maximum_fusion.1.refs_4_), channel_id=1, source_target_pairs={{0,64},{1,193},{2,66},{3,195},{4,68},{5,197},{6,70},{7,199},{8,72}... | collective-permute-start | bytes 2359304 | tf_op jit(solution)/shard_map/ppermute | solution.py:243
  46.0 0.9 copy-start.11
  46.0 13.2 %collective-permute-start.4 = (bf16[4,2,128,384]{3,2,1,0:T(8,128)(2,1)S(1)}, bf16[4,2,128,384]{3,2,1,0:T(8,128)(2,1)S(1)}, u32[]{:S(2)}, u32[]{:S(2)}) collective-permute-start(bf16[4,2,128,384]{3,2,1,0:T(8,128)(2,1)S(1)} %collective-permute-done.3.refs_1_), channel_id=1, source_target_pairs={{0,16},{1,49},{2,18},{3,51},{4,20},{5,53},{6,22},{7,55},{8,24},{9,... | collective-permute-start | bytes 2359304 | tf_op jit(solution)/shard_map/ppermute | solution.py:243
  46.9 12.3 %copy-start.12 = (bf16[4,2,128,384]{3,2,1,0:T(8,128)(2,1)}, bf16[4,2,128,384]{3,2,1,0:T(8,128)(2,1)S(1)}, u32[]{:S(2)}) copy-start(bf16[4,2,128,384]{3,2,1,0:T(8,128)(2,1)S(1)} %collective-permute-done.9.refs_5_) | copy-start | bytes 2359300
  46.9 12.3 %collective-permute-start.10 = (bf16[4,2,128,384]{3,2,1,0:T(8,128)(2,1)S(1)}, bf16[4,2,128,384]{3,2,1,0:T(8,128)(2,1)S(1)}, u32[]{:S(2)}, u32[]{:S(2)}) collective-permute-start(bf16[4,2,128,384]{3,2,1,0:T(8,128)(2,1)S(1)} %collective-permute-done.9.refs_5_), channel_id=1, source_target_pairs={{0,64},{1,193},{2,66},{3,195},{4,68},{5,197},{6,70},{7,199},{8,72}... | collective-permute-start | bytes 2359304 | tf_op jit(solution)/shard_map/ppermute | solution.py:243
  59.2 48.8 %copy-start.13 = (bf16[4,2,128,384]{3,2,1,0:T(8,128)(2,1)}, bf16[4,2,128,384]{3,2,1,0:T(8,128)(2,1)S(1)}, u32[]{:S(2)}) copy-start(bf16[4,2,128,384]{3,2,1,0:T(8,128)(2,1)S(1)} %collective-permute-done.4.refs_2_) | copy-start | bytes 2359300
  59.2 16.8 %collective-permute-start.5 = (bf16[4,2,128,384]{3,2,1,0:T(8,128)(2,1)S(1)}, bf16[4,2,128,384]{3,2,1,0:T(8,128)(2,1)}, u32[]{:S(2)}, u32[]{:S(2)}) collective-permute-start(bf16[4,2,128,384]{3,2,1,0:T(8,128)(2,1)S(1)} %collective-permute-done.4.refs_2_), channel_id=1, source_target_pairs={{0,16},{1,49},{2,18},{3,51},{4,20},{5,53},{6,22},{7,55},{8,24},{9,... | collective-permute-start | bytes 2359304 | tf_op jit(solution)/shard_map/ppermute | solution.py:243
  59.2 48.8 %copy-start.14 = (bf16[4,2,128,384]{3,2,1,0:T(8,128)(2,1)}, bf16[4,2,128,384]{3,2,1,0:T(8,128)(2,1)S(1)}, u32[]{:S(2)}) copy-start(bf16[4,2,128,384]{3,2,1,0:T(8,128)(2,1)S(1)} %collective-permute-done.10.refs_6_) | copy-start | bytes 2359300
  59.3 16.7 %collective-permute-start.11 = (bf16[4,2,128,384]{3,2,1,0:T(8,128)(2,1)S(1)}, bf16[4,2,128,384]{3,2,1,0:T(8,128)(2,1)}, u32[]{:S(2)}, u32[]{:S(2)}) collective-permute-start(bf16[4,2,128,384]{3,2,1,0:T(8,128)(2,1)S(1)} %collective-permute-done.10.refs_6_), channel_id=1, source_target_pairs={{0,64},{1,193},{2,66},{3,195},{4,68},{5,197},{6,70},{7,199},{8,72}... | collective-permute-start | bytes 2359304 | tf_op jit(solution)/shard_map/ppermute | solution.py:243
  108.0 20.0 %collective-permute-start.12 = (bf16[2,4,384,128]{3,2,1,0:T(8,128)(2,1)}, bf16[2,4,384,128]{3,2,1,0:T(8,128)(2,1)S(1)}, u32[]{:S(2)}, u32[]{:S(2)}) collective-permute-start(bf16[2,4,384,128]{3,2,1,0:T(8,128)(2,1)} %get-tuple-element.30), channel_id=1, source_target_pairs={{0,64},{1,65},{2,66},{3,67},{4,68},{5,69},{6,70},{7,71},{8,72},{9,... | collective-permute-start | bytes 2359304 | tf_op jit(solution)/shard_map/ppermute | solution.py:243
  108.6 20.8 %collective-permute-start.13 = (bf16[2,4,384,128]{3,2,1,0:T(8,128)(2,1)}, bf16[2,4,384,128]{3,2,1,0:T(8,128)(2,1)S(1)}, u32[]{:S(2)}, u32[]{:S(2)}) collective-permute-start(bf16[2,4,384,128]{3,2,1,0:T(8,128)(2,1)} %get-tuple-element.31), channel_id=1, source_target_pairs={{0,192},{1,193},{2,194},{3,195},{4,196},{5,197},{6,198},{7,199},{8... | collective-permute-start | bytes 2359304 | tf_op jit(solution)/shard_map/ppermute | solution.py:243
  110.1 24.3 %collective-permute-start.16 = (bf16[2,4,384,128]{3,2,1,0:T(8,128)(2,1)}, bf16[2,4,384,128]{3,2,1,0:T(8,128)(2,1)S(1)}, u32[]{:S(2)}, u32[]{:S(2)}) collective-permute-start(bf16[2,4,384,128]{3,2,1,0:T(8,128)(2,1)} %get-tuple-element.34), channel_id=1, source_target_pairs={{0,16},{1,17},{2,18},{3,19},{4,20},{5,21},{6,22},{7,23},{8,24},{9,... | collective-permute-start | bytes 2359304 | tf_op jit(solution)/shard_map/ppermute | solution.py:243
  111.6 22.8 %collective-permute-start.17 = (bf16[2,4,384,128]{3,2,1,0:T(8,128)(2,1)}, bf16[2,4,384,128]{3,2,1,0:T(8,128)(2,1)}, u32[]{:S(2)}, u32[]{:S(2)}) collective-permute-start(bf16[2,4,384,128]{3,2,1,0:T(8,128)(2,1)} %get-tuple-element.35), channel_id=1, source_target_pairs={{0,48},{1,49},{2,50},{3,51},{4,52},{5,53},{6,54},{7,55},{8,56},{9,... | collective-permute-start | bytes 2359304 | tf_op jit(solution)/shard_map/ppermute | solution.py:243
  121.3 40.5 %all-to-all-start.1 = ((bf16[16,96,384]{2,1,0:T(8,128)(2,1)}), bf16[16,96,384]{2,1,0:T(8,128)(2,1)S(1)}, u32[]{:S(2)}, u32[]{:S(2)}) async-start(bf16[16,96,384]{2,1,0:T(8,128)(2,1)} %hidden_grad.1), calls=%async_computation.1 | async-start | bytes 2359296 | tf_op jit(solution)/shard_map/all_to_all | solution.py:407
  125.8 8.7 %copy-start.10 = (bf16[2,4,384,128]{3,2,1,0:T(8,128)(2,1)S(1)}, bf16[2,4,384,128]{3,2,1,0:T(8,128)(2,1)}, u32[]{:S(2)}) copy-start(bf16[2,4,384,128]{3,2,1,0:T(8,128)(2,1)} %get-tuple-element.36) | copy-start | bytes 2359300
  130.8 18.3 %copy-start.6 = (bf16[2,4,384,128]{3,2,1,0:T(8,128)(2,1)S(1)}, bf16[2,4,384,128]{3,2,1,0:T(8,128)(2,1)}, u32[]{:S(2)}) copy-start(bf16[2,4,384,128]{3,2,1,0:T(8,128)(2,1)} %get-tuple-element.29.refs_0_) | copy-start | bytes 2359300
  130.9 18.3 %copy-start.7 = (bf16[2,4,384,128]{3,2,1,0:T(8,128)(2,1)S(1)}, bf16[2,4,384,128]{3,2,1,0:T(8,128)(2,1)}, u32[]{:S(2)}) copy-start(bf16[2,4,384,128]{3,2,1,0:T(8,128)(2,1)} %get-tuple-element.33.refs_5_) | copy-start | bytes 2359300
  130.9 11.6 %collective-permute-start.15 = (bf16[4,384,128]{2,1,0:T(8,128)(2,1)S(1)}, bf16[4,384,128]{2,1,0:T(8,128)(2,1)S(1)}, u32[]{:S(2)}, u32[]{:S(2)}) collective-permute-start(bf16[4,384,128]{2,1,0:T(8,128)(2,1)S(1)} %get-tuple-element.47), channel_id=1, source_target_pairs={{0,192},{1,193},{2,194},{3,195},{4,196},{5,197},{6,198},{7,199},{8... | collective-permute-start | bytes 1179656 | tf_op jit(solution)/shard_map/ppermute | solution.py:243
  131.4 11.1 %collective-permute-start.14 = (bf16[4,384,128]{2,1,0:T(8,128)(2,1)S(1)}, bf16[4,384,128]{2,1,0:T(8,128)(2,1)S(1)}, u32[]{:S(2)}, u32[]{:S(2)}) collective-permute-start(bf16[4,384,128]{2,1,0:T(8,128)(2,1)S(1)} %get-tuple-element.48), channel_id=1, source_target_pairs={{0,64},{1,65},{2,66},{3,67},{4,68},{5,69},{6,70},{7,71},{8,72},{9,... | collective-permute-start | bytes 1179656 | tf_op jit(solution)/shard_map/ppermute | solution.py:243
  135.7 10.0 %collective-permute-start.19 = (bf16[4,384,128]{2,1,0:T(8,128)(2,1)S(1)}, bf16[4,384,128]{2,1,0:T(8,128)(2,1)S(1)}, u32[]{:S(2)}, u32[]{:S(2)}) collective-permute-start(bf16[4,384,128]{2,1,0:T(8,128)(2,1)S(1)} %get-tuple-element.45), channel_id=1, source_target_pairs={{0,48},{1,49},{2,50},{3,51},{4,52},{5,53},{6,54},{7,55},{8,56},{9,... | collective-permute-start | bytes 1179656 | tf_op jit(solution)/shard_map/ppermute | solution.py:243
  138.5 10.6 %collective-permute-start.18 = (bf16[4,384,128]{2,1,0:T(8,128)(2,1)S(1)}, bf16[4,384,128]{2,1,0:T(8,128)(2,1)S(1)}, u32[]{:S(2)}, u32[]{:S(2)}) collective-permute-start(bf16[4,384,128]{2,1,0:T(8,128)(2,1)S(1)} %get-tuple-element.46), channel_id=1, source_target_pairs={{0,16},{1,17},{2,18},{3,19},{4,20},{5,21},{6,22},{7,23},{8,24},{9,... | collective-permute-start | bytes 1179656 | tf_op jit(solution)/shard_map/ppermute | solution.py:243
  152.1 9.8 %collective-permute-start.20 = (bf16[2,384,128]{2,1,0:T(8,128)(2,1)S(1)}, bf16[2,384,128]{2,1,0:T(8,128)(2,1)S(1)}, u32[]{:S(2)}, u32[]{:S(2)}) collective-permute-start(bf16[2,384,128]{2,1,0:T(8,128)(2,1)S(1)} %get-tuple-element.38), channel_id=1, source_target_pairs={{0,16},{1,17},{2,18},{3,19},{4,20},{5,21},{6,22},{7,23},{8,24},{9,... | collective-permute-start | bytes 589832 | tf_op jit(solution)/shard_map/ppermute | solution.py:243
  152.2 14.0 %collective-permute-start.21 = (bf16[2,384,128]{2,1,0:T(8,128)(2,1)}, bf16[2,384,128]{2,1,0:T(8,128)(2,1)S(1)}, u32[]{:S(2)}, u32[]{:S(2)}) collective-permute-start(bf16[2,384,128]{2,1,0:T(8,128)(2,1)} %get-tuple-element.39), channel_id=1, source_target_pairs={{0,32},{1,33},{2,34},{3,35},{4,36},{5,37},{6,38},{7,39},{8,40},{9,... | collective-permute-start | bytes 589832 | tf_op jit(solution)/shard_map/ppermute | solution.py:243
  153.9 12.2 %collective-permute-start.22 = (bf16[2,384,128]{2,1,0:T(8,128)(2,1)}, bf16[2,384,128]{2,1,0:T(8,128)(2,1)S(1)}, u32[]{:S(2)}, u32[]{:S(2)}) collective-permute-start(bf16[2,384,128]{2,1,0:T(8,128)(2,1)} %get-tuple-element.40), channel_id=1, source_target_pairs={{0,48},{1,49},{2,50},{3,51},{4,52},{5,53},{6,54},{7,55},{8,56},{9,... | collective-permute-start | bytes 589832 | tf_op jit(solution)/shard_map/ppermute | solution.py:243
  155.4 10.8 %collective-permute-start.23 = (bf16[2,384,128]{2,1,0:T(8,128)(2,1)}, bf16[2,384,128]{2,1,0:T(8,128)(2,1)S(1)}, u32[]{:S(2)}, u32[]{:S(2)}) collective-permute-start(bf16[2,384,128]{2,1,0:T(8,128)(2,1)} %get-tuple-element.42), channel_id=1, source_target_pairs={{0,64},{1,65},{2,66},{3,67},{4,68},{5,69},{6,70},{7,71},{8,72},{9,... | collective-permute-start | bytes 589832 | tf_op jit(solution)/shard_map/ppermute | solution.py:243
  155.7 10.5 %collective-permute-start.24 = (bf16[2,384,128]{2,1,0:T(8,128)(2,1)}, bf16[2,384,128]{2,1,0:T(8,128)(2,1)S(1)}, u32[]{:S(2)}, u32[]{:S(2)}) collective-permute-start(bf16[2,384,128]{2,1,0:T(8,128)(2,1)} %get-tuple-element.43), channel_id=1, source_target_pairs={{0,128},{1,129},{2,130},{3,131},{4,132},{5,133},{6,134},{7,135},{8... | collective-permute-start | bytes 589832 | tf_op jit(solution)/shard_map/ppermute | solution.py:243
  161.8 7.1 %collective-permute-start.25 = (bf16[2,384,128]{2,1,0:T(8,128)(2,1)}, bf16[2,384,128]{2,1,0:T(8,128)(2,1)S(1)}, u32[]{:S(2)}, u32[]{:S(2)}) collective-permute-start(bf16[2,384,128]{2,1,0:T(8,128)(2,1)} %get-tuple-element.44), channel_id=1, source_target_pairs={{0,192},{1,193},{2,194},{3,195},{4,196},{5,197},{6,198},{7,199},{8... | collective-permute-start | bytes 589832 | tf_op jit(solution)/shard_map/ppermute | solution.py:243
  161.9 1.1 copy-start.3
  163.0 6.0 %copy-start = (bf16[2,384,128]{2,1,0:T(8,128)(2,1)S(1)}, bf16[2,384,128]{2,1,0:T(8,128)(2,1)}, u32[]{:S(2)}) copy-start(bf16[2,384,128]{2,1,0:T(8,128)(2,1)} %get-tuple-element.37.refs_0_) | copy-start | bytes 589828
  163.0 6.0 %copy-start.1 = (bf16[2,384,128]{2,1,0:T(8,128)(2,1)S(1)}, bf16[2,384,128]{2,1,0:T(8,128)(2,1)}, u32[]{:S(2)}) copy-start(bf16[2,384,128]{2,1,0:T(8,128)(2,1)} %get-tuple-element.41.refs_4_) | copy-start | bytes 589828
Sparse Core Ops, SparseCore 0:
  9.9 86.1 all-gather.2
